TPU v7x, 128 devices: a whole 4x4x4 slice. The times are simulated.
128 devices in a mesh: swath: 8 (over y, core), seg: 16 (over z, x).
Axes of the slice: x: 4, y: 4, z: 4, core: 2. Of those that a mesh axis runs over, the one named last changes fastest.
Arguments:
- swath_pixels: bfloat16 [8, 16, 128, 1024], P('swath', 'seg'), may hold values from -6 to 6
- stencils: float32 [8, 2, 9], replicated, may hold values from -6 to 6
- classes: int32 [16, 16, 32], P('seg', 'swath'), may hold values from 0 to 7
- neighbours: int32 [16, 16, 2], P('seg'), may hold values from 0 to 15, as said below
Outputs:
- responses: bfloat16 [16, 4, 8, 128, 1024], P('seg', None, None, 'swath')
Inputs may be any that keep to these rules, and one draw needn't show every extreme that they name: `neighbours`: the two entries of a row block of die j are different dies, each other than j.
All inputs are finite; a program needn't handle non-finite values.
Results may differ from a plain program's by a relative error of at most 0.0049.
Values may be sent and summed in bfloat16 or wider, within the bound.
No kernel may reach another device: no remote copies, remote signals or barrier semaphores. Data moves between devices by JAX's collectives and lax.ppermute only.
A program may use at most 64 MiB of HBM per device.

v0:
```python
import functools

import jax
import jax.numpy as jnp
from jax import lax
from jax.experimental import pallas as pl
from jax.experimental.pallas import tpu as pltpu
from jax.sharding import PartitionSpec as P

CH = 2
BLK_R = 8
BLK_C = 128
NCLASS = 8
SWATHS = 8
DIES = 16
ROWS = 128
COLS = 512
BAND = 16
PARTS = 16
COL_BLOCKS = SWATHS * COLS // BLK_C
WIDE = SWATHS * COLS + 2 * BLK_C
PIECE = COLS + BLK_C
VMEM_LIMIT = 24 * 1024 * 1024

TAPS = (-0.5, 0.25, 1.0, 0.25, -0.5)


def rows_of(count, width):
    return lax.broadcasted_iota(jnp.int32, (count, width), 0)


def pack_kernel(pix_ref, cls_ref, out_ref, row_ref):
    row_ref[...] = jnp.zeros_like(row_ref)
    row_ref[6:8, 0:COL_BLOCKS] = cls_ref[...].astype(jnp.float32)
    own_classes = row_ref[...]
    sub = rows_of(8, COLS)
    for band in range(SWATHS):
        start = band * BAND
        out_ref[band, :, 0 : CH * COLS] = pix_ref[start : start + BAND, :]
        for h in range(CH):
            lanes = slice(h * COLS, (h + 1) * COLS)
            if band > 0:
                above = pix_ref[start - BAND : start, lanes].astype(jnp.float32)[8:16]
                above = pltpu.roll(above, 3, 0)
            else:
                above = jnp.zeros((8, COLS), jnp.float32)
            if band < SWATHS - 1:
                below = pix_ref[start + BAND : start + 2 * BAND, lanes].astype(jnp.float32)[0:8]
                below = pltpu.roll(below, 3, 0)
            else:
                below = jnp.zeros((8, COLS), jnp.float32)
            halo = jnp.where(sub < 3, above, jnp.where(sub < 6, below, own_classes))
            if h == 0:
                first = halo
        out_ref[band, :, CH * COLS :] = jnp.concatenate([first, halo], axis=0).astype(jnp.bfloat16)


def norm_kernel(band, recv_ref, sten_ref, out_ref, image_ref, cls_v, cls_s, sem):
    if band is None:
        band = lax.axis_index("swath")
    before = jnp.maximum(band - 1, 0)
    after = jnp.minimum(band + 1, SWATHS - 1)

    def class_rows(source):
        return recv_ref[source, :, CH * COLS : CH * COLS + BLK_C].astype(jnp.float32)[0:8].astype(jnp.int32)

    cls_v[0:8] = class_rows(before)
    cls_v[8:16] = class_rows(band)
    cls_v[16:24] = class_rows(after)
    copy = pltpu.make_async_copy(cls_v, cls_s, sem)
    copy.start()

    for h in range(CH):
        image_ref[h, :, 0:BLK_C] = jnp.zeros((24, BLK_C), jnp.float32)
        image_ref[h, :, WIDE - BLK_C : WIDE] = jnp.zeros((24, BLK_C), jnp.float32)
        for g in range(SWATHS):
            lanes = slice(BLK_C + g * COLS, BLK_C + (g + 1) * COLS)
            image_ref[h, 0:16, lanes] = recv_ref[g, :, h * COLS : (h + 1) * COLS].astype(jnp.float32)
            halo = recv_ref[g, :, CH * COLS :].astype(jnp.float32)[h * 8 : h * 8 + 8]
            image_ref[h, 16:24, lanes] = pltpu.roll(halo, 5, 0)
    copy.wait()

    top = jnp.where(band > 0, 1.0, 0.0)
    bottom = jnp.where(band < SWATHS - 1, 1.0, 0.0)
    sub = rows_of(8, BLK_C)

    def step(g, carry):
        for h in range(CH):
            base = pl.multiple_of(g * COLS, COLS)
            window = image_ref[h, :, pl.ds(base, COLS + 2 * BLK_C)]
            wide = COLS + 2 * BLK_C
            cols = [
                pltpu.roll(window, 1, 1)[:, BLK_C : BLK_C + COLS],
                window[:, BLK_C : BLK_C + COLS],
                pltpu.roll(window, wide - 1, 1)[:, BLK_C : BLK_C + COLS],
            ]
            shifted = [[pltpu.roll(c, 1, 0), c, pltpu.roll(c, 23, 0)] for c in cols]
            above = jnp.zeros((8, BLK_C), jnp.float32)
            below = jnp.zeros((8, BLK_C), jnp.float32)
            for q in range(COLS // BLK_C):
                block = g * (COLS // BLK_C) + q
                offsets = [
                    (cls_s[row, block] * CH + h) * 9 for row in (7, 14, 15, 22)
                ]
                total = [jnp.zeros((8, BLK_C), jnp.float32) for _ in range(3)]
                lanes = slice(q * BLK_C, (q + 1) * BLK_C)
                for dr in range(3):
                    for dc in range(3):
                        k = 3 * dr + dc
                        coefs = [sten_ref[offset + k] for offset in offsets]
                        source = shifted[dc][dr]
                        edge = jnp.where(sub < 4, coefs[3] * bottom, coefs[0] * top)
                        total[0] = total[0] + coefs[1] * source[0:8, lanes]
                        total[1] = total[1] + coefs[2] * source[8:16, lanes]
                        total[2] = total[2] + edge * source[16:24, lanes]
                out_ref[2 * g + h, :, lanes] = jnp.concatenate(total[:2], axis=0).astype(jnp.bfloat16)
                mine = (sub // 2) == q
                above = jnp.where(mine, pltpu.roll(total[2], (2 * q + 2) % 8, 0), above)
                below = jnp.where(mine, pltpu.roll(total[2], 2 * q, 0) if q else total[2], below)
            out_ref[2 * g + h, :, COLS:] = jnp.concatenate([above, below], axis=0).astype(jnp.bfloat16)
        return carry

    lax.fori_loop(0, SWATHS, step, 0)


def pick_kernel(band, near_ref, recv_ref, out_ref):
    if band is None:
        band = lax.axis_index("swath")
    blocks = ROWS // BLK_R
    first = band * 2
    rows = (jnp.maximum(first - 1, 0), first, first + 1, jnp.minimum(first + 2, blocks - 1))
    main_top = rows_of(16, COLS) < 8
    edge_top = rows_of(16, BLK_C) < 8
    for die in range(DIES):
        for k in range(2):
            up, one, two, down = [near_ref[(die * blocks + row) * 2 + k] for row in rows]
            out_ref[2 * die + k, :, 0:COLS] = jnp.where(
                main_top, recv_ref[one, :, 0:COLS], recv_ref[two, :, 0:COLS]
            )
            out_ref[2 * die + k, :, COLS:] = jnp.where(
                edge_top, recv_ref[up, :, COLS:], recv_ref[down, :, COLS:]
            )


def unpack_edge(edge):
    sub = rows_of(8, BLK_C)
    tiles = []
    for q in range(COLS // BLK_C):
        above = pltpu.roll(edge[0:8], (6 - 2 * q) % 8, 0) if q != 3 else edge[0:8]
        below = pltpu.roll(edge[8:16], (8 - 2 * q) % 8, 0) if q else edge[8:16]
        tiles.append(jnp.where(sub < 4, below, above))
    return jnp.concatenate(tiles, axis=1)


def filter_kernel(own_ref, near_ref, out_ref, differ_ref):
    for h in range(CH):
        for k in range(2):
            differ_ref[h, k, :, 0:BLK_C] = jnp.zeros((24, BLK_C), jnp.float32)
            differ_ref[h, k, :, WIDE - BLK_C : WIDE] = jnp.zeros((24, BLK_C), jnp.float32)

    def fill(g, carry):
        base = pl.multiple_of(BLK_C + g * COLS, BLK_C)
        for h in range(CH):
            part = 2 * g + h
            own = own_ref[part].astype(jnp.float32)
            for k in range(2):
                differ = own - near_ref[2 * part + k].astype(jnp.float32)
                differ_ref[h, k, 0:16, pl.ds(base, COLS)] = differ[:, 0:COLS]
                differ_ref[h, k, 16:24, pl.ds(base, COLS)] = unpack_edge(differ[:, COLS:])
        return carry

    lax.fori_loop(0, SWATHS, fill, 0)

    wide = COLS + 2 * BLK_C

    def step(g, carry):
        base = pl.multiple_of(g * COLS, COLS)
        for h in range(CH):
            lowest = None
            for k in range(2):
                window = differ_ref[h, k, :, pl.ds(base, wide)]
                cols = {}
                for t in (-2, -1, 1, 2):
                    cols[t] = pltpu.roll(window, (-t) % wide, 1)[:, BLK_C : BLK_C + COLS]
                middle = window[:, BLK_C : BLK_C + COLS]

                def row(value, t):
                    return pltpu.roll(value, (-t) % 24, 0)[0:16]

                def combine(m2, m1, p1, p2):
                    return middle[0:16] + 0.25 * (m1 + p1) - 0.5 * (m2 + p2)

                found = [
                    combine(*[cols[t][0:16] for t in (-2, -1, 1, 2)]),
                    combine(*[row(middle, t) for t in (-2, -1, 1, 2)]),
                    combine(*[row(cols[t], t) for t in (-2, -1, 1, 2)]),
                    combine(*[row(cols[-t], t) for t in (-2, -1, 1, 2)]),
                ]
                lowest = found if lowest is None else [jnp.minimum(a, b) for a, b in zip(lowest, found)]
            for d in range(4):
                out_ref[d, g, :, h * COLS : (h + 1) * COLS] = lowest[d].astype(jnp.bfloat16)
        return carry

    lax.fori_loop(0, SWATHS, step, 0)


VMEM = pl.BlockSpec(memory_space=pltpu.VMEM)
SMEM = pl.BlockSpec(memory_space=pltpu.SMEM)
PARAMS = pltpu.CompilerParams(vmem_limit_bytes=VMEM_LIMIT)


def pack(pixels, classes, interpret=False):
    return pl.pallas_call(
        pack_kernel,
        out_shape=jax.ShapeDtypeStruct((SWATHS, BAND, 3 * COLS), jnp.bfloat16),
        in_specs=[VMEM, VMEM],
        out_specs=VMEM,
        scratch_shapes=[pltpu.VMEM((8, COLS), jnp.float32)],
        compiler_params=PARAMS,
        interpret=interpret,
    )(pixels, classes)


def norm(recv, stencils, band=None, interpret=False):
    return pl.pallas_call(
        functools.partial(norm_kernel, band),
        out_shape=jax.ShapeDtypeStruct((PARTS, BAND, PIECE), jnp.bfloat16),
        in_specs=[VMEM, SMEM],
        out_specs=VMEM,
        scratch_shapes=[
            pltpu.VMEM((CH, 24, WIDE), jnp.float32),
            pltpu.VMEM((24, BLK_C), jnp.int32),
            pltpu.SMEM((24, BLK_C), jnp.int32),
            pltpu.SemaphoreType.DMA,
        ],
        compiler_params=PARAMS,
        interpret=interpret,
    )(recv, stencils)


def pick(near, recv, band=None, interpret=False):
    return pl.pallas_call(
        functools.partial(pick_kernel, band),
        out_shape=jax.ShapeDtypeStruct((2 * DIES, BAND, PIECE), jnp.bfloat16),
        in_specs=[SMEM, VMEM],
        out_specs=VMEM,
        compiler_params=PARAMS,
        interpret=interpret,
    )(near, recv)


def filters(own, near, interpret=False):
    return pl.pallas_call(
        filter_kernel,
        out_shape=jax.ShapeDtypeStruct((4, SWATHS, BAND, CH * COLS), jnp.bfloat16),
        in_specs=[VMEM, VMEM],
        out_specs=VMEM,
        scratch_shapes=[pltpu.VMEM((CH, 2, 24, WIDE), jnp.float32)],
        compiler_params=PARAMS,
        interpret=interpret,
    )(own, near)


def shards(swath_pixels, stencils, classes, neighbours):
    near = lax.all_gather(neighbours.reshape(-1), "seg", axis=0, tiled=True)
    packed = pack(swath_pixels[0, 0], classes[0])
    bands = lax.all_to_all(packed, "swath", split_axis=0, concat_axis=0, tiled=True)
    own = norm(bands, stencils.reshape(-1))
    pieces = lax.all_to_all(own, "seg", split_axis=0, concat_axis=0, tiled=True)
    picked = pick(near, pieces)
    references = lax.all_to_all(picked, "seg", split_axis=0, concat_axis=0, tiled=True)
    return filters(own, references)[None]


def solution(mesh):
    return jax.shard_map(
        shards,
        mesh=mesh,
        in_specs=(
            P("swath", "seg", None, None),
            P(),
            P("seg", "swath", None),
            P("seg", None, None),
        ),
        out_specs=P("seg", None, None, "swath", None),
        check_vma=False,
    )
```

profile of v0, /device:TPU:0, one launch (start us, length us, event | category | flops | bytes accessed | tf_op | source)
XLA Modules:
  0.0 67.5 jit_solution(15197047985799230004)
XLA Ops:
  0.0 0.0 copy-start.1
  0.0 0.7 %copy-done.1 = s32[1,2,32]{2,1,0:T(2,128)S(1)} copy-done((s32[1,2,32]{2,1,0:T(2,128)S(1)}, s32[1,2,32]{2,1,0:T(2,128)}, u32[]{:S(2)}) %copy-start.1) | copy-done | bytes 280
  0.7 0.0 copy-start
  0.7 0.9 %copy-done = bf16[1,1,128,1024]{3,2,1,0:T(8,128)(2,1)S(1)} copy-done((bf16[1,1,128,1024]{3,2,1,0:T(8,128)(2,1)S(1)}, bf16[1,1,128,1024]{3,2,1,0:T(8,128)(2,1)}, u32[]{:S(2)}) %copy-start) | copy-done | bytes 262168
  1.6 0.8 %shard_map.46 = bf16[8,16,1536]{2,1,0:T(8,128)(2,1)} custom-call(bf16[128,1024]{1,0:T(8,128)(2,1)S(1)} %bitcast.4, s32[2,32]{1,0:T(2,128)S(1)} %bitcast.5), custom_call_target="tpu_custom_call" | custom-call | tf_op jit(solution)/shard_map/pallas_call | solution.py:213
  2.4 0.0 copy-start.2
  2.4 4.7 %all-to-all-start = ((bf16[8,16,1536]{2,1,0:T(8,128)(2,1)}), bf16[8,16,1536]{2,1,0:T(8,128)(2,1)S(1)}, u32[]{:S(2)}, u32[]{:S(2)}) async-start(bf16[8,16,1536]{2,1,0:T(8,128)(2,1)} %shard_map.46), calls=%async_computation | async-start | bytes 786432 | tf_op jit(solution)/shard_map/all_to_all | solution.py:267
  7.1 0.0 copy-done.2
  7.1 0.1 reshape.6.sten_ref
  7.2 8.8 %all-to-all-done.recv_ref = bf16[8,16,1536]{2,1,0:T(8,128)(2,1)S(1)} async-done(((bf16[8,16,1536]{2,1,0:T(8,128)(2,1)}), bf16[8,16,1536]{2,1,0:T(8,128)(2,1)S(1)}, u32[]{:S(2)}, u32[]{:S(2)}) %all-to-all-start) | async-done | bytes 393248 | tf_op jit(solution)/shard_map/all_to_all | solution.py:267
  16.1 4.9 %shard_map.47.own_ref = bf16[16,16,640]{2,1,0:T(8,128)(2,1)} custom-call(bf16[8,16,1536]{2,1,0:T(8,128)(2,1)S(1)} %all-to-all-done.recv_ref, f32[144]{0:T(256)S(1)} %reshape.6.sten_ref), custom_call_target="tpu_custom_call" | custom-call | tf_op jit(solution)/shard_map/pallas_call | solution.py:225
  20.9 7.9 %all-to-all-start.1 = ((bf16[16,16,640]{2,1,0:T(8,128)(2,1)}), bf16[16,16,640]{2,1,0:T(8,128)(2,1)S(1)}, u32[]{:S(2)}, u32[]{:S(2)}) async-start(bf16[16,16,640]{2,1,0:T(8,128)(2,1)} %shard_map.47.own_ref), calls=%async_computation.1 | async-start | bytes 655360 | tf_op jit(solution)/shard_map/all_to_all | solution.py:269
  28.9 0.0 copy-start.3
  28.9 0.7 copy-done.3
  29.5 0.1 copy.6
  29.6 0.1 reshape.8
  29.7 0.0 copy-start.4
  29.7 0.6 copy-done.4
  30.4 0.6 dynamic-slice
  31.6 0.2 dynamic-update-slice
  31.9 16.6 %all-reduce.near_ref = s32[512]{0:T(512)S(1)} all-reduce(s32[512]{0:T(512)S(1)} %dynamic-update-slice), channel_id=1, replica_groups=mesh['swath'=8,'seg'=16] {'seg'}, use_global_device_ids=true, to_apply=%add | all-reduce | flops 512 | bytes 4096
  48.5 0.0 all-to-all-done.1.recv_ref
  48.5 0.7 %shard_map.48 = bf16[32,16,640]{2,1,0:T(8,128)(2,1)S(1)} custom-call(s32[512]{0:T(512)S(1)} %all-reduce.near_ref, bf16[16,16,640]{2,1,0:T(8,128)(2,1)S(1)} %all-to-all-done.1.recv_ref), custom_call_target="tpu_custom_call" | custom-call | tf_op jit(solution)/shard_map/pallas_call | solution.py:242
  49.2 13.5 %all_to_all.15.near_ref = bf16[32,16,640]{2,1,0:T(8,128)(2,1)S(1)} all-to-all(bf16[32,16,640]{2,1,0:T(8,128)(2,1)S(1)} %shard_map.48), channel_id=1, replica_groups=mesh['swath'=8,'seg'=16] {'seg'}, dimensions={0} | all-to-all | bytes 1310720 | tf_op jit(solution)/shard_map/all_to_all | solution.py:271
  62.7 4.8 %shard_map.49 = bf16[4,8,16,1024]{3,2,1,0:T(8,128)(2,1)} custom-call(bf16[16,16,640]{2,1,0:T(8,128)(2,1)} %shard_map.47.own_ref, bf16[32,16,640]{2,1,0:T(8,128)(2,1)S(1)} %all_to_all.15.near_ref), custom_call_target="tpu_custom_call" | custom-call | tf_op jit(solution)/shard_map/pallas_call | solution.py:253
  (1 shorter events, 0.0 us)
Async XLA Ops:
  0.0 0.7 %copy-start.1 = (s32[1,2,32]{2,1,0:T(2,128)S(1)}, s32[1,2,32]{2,1,0:T(2,128)}, u32[]{:S(2)}) copy-start(s32[1,2,32]{2,1,0:T(2,128)} %param.6) | copy-start | bytes 772
  0.7 0.9 %copy-start = (bf16[1,1,128,1024]{3,2,1,0:T(8,128)(2,1)S(1)}, bf16[1,1,128,1024]{3,2,1,0:T(8,128)(2,1)}, u32[]{:S(2)}) copy-start(bf16[1,1,128,1024]{3,2,1,0:T(8,128)(2,1)} %param.4) | copy-start | bytes 786436
  2.4 4.7 %copy-start.2 = (f32[8,2,9]{2,1,0:T(2,128)S(1)}, f32[8,2,9]{2,1,0:T(2,128)}, u32[]{:S(2)}) copy-start(f32[8,2,9]{2,1,0:T(2,128)} %param.5) | copy-start | bytes 1732
  2.4 13.6 %all-to-all-start = ((bf16[8,16,1536]{2,1,0:T(8,128)(2,1)}), bf16[8,16,1536]{2,1,0:T(8,128)(2,1)S(1)}, u32[]{:S(2)}, u32[]{:S(2)}) async-start(bf16[8,16,1536]{2,1,0:T(8,128)(2,1)} %shard_map.46), calls=%async_computation | async-start | bytes 786432 | tf_op jit(solution)/shard_map/all_to_all | solution.py:267
  20.9 27.5 %all-to-all-start.1 = ((bf16[16,16,640]{2,1,0:T(8,128)(2,1)}), bf16[16,16,640]{2,1,0:T(8,128)(2,1)S(1)}, u32[]{:S(2)}, u32[]{:S(2)}) async-start(bf16[16,16,640]{2,1,0:T(8,128)(2,1)} %shard_map.47.own_ref), calls=%async_computation.1 | async-start | bytes 655360 | tf_op jit(solution)/shard_map/all_to_all | solution.py:269
  28.9 0.7 %copy-start.3 = (s32[1,16,2]{1,2,0:T(2,128)S(1)}, s32[1,16,2]{1,2,0:T(2,128)}, u32[]{:S(2)}) copy-start(s32[1,16,2]{1,2,0:T(2,128)} %param.7) | copy-start | bytes 388
  29.7 0.7 copy-start.4
where the time goes:
time: 68 us; the launch traced here: 67.5 us
  blocking collectives  30.1 us (44%)
  starting transfers between devices  12.6 us (19%)
  Pallas kernels  11.2 us (16%)
  waiting for transfers between devices  8.85 us (13%)
  local copies, waits for them, and re-layouts  4.04 us (6%)
  between operations  0.73 us (1%)
    unnamed x1, blocking collectives  16.6 us
    all_to_all x1, blocking collectives, shards(): lax.all_to_all(picked, 'seg', split_axis=0, concat_axis=0, tiled=True)  13.5 us
    all_to_all x1, waiting for transfers between devices, shards(): lax.all_to_all(packed, 'swath', split_axis=0, concat_axis=0, tiled=True)  8.84 us
    all_to_all x1, starting transfers between devices, shards(): pieces = lax.all_to_all(own, 'seg', split_axis=0, concat_axis=0, tiled=True)  7.89 us
    pallas_call x1, Pallas kernels, norm(): pl.pallas_call(functools.partial(norm_kernel, band), out_shape=jax.ShapeD...  4.87 us
    pallas_call x1, Pallas kernels, filters(): pl.pallas_call(filter_kernel, out_shape=jax.ShapeDtypeStruct((4, SWATHS,...  4.82 us
    all_to_all x1, starting transfers between devices, shards(): lax.all_to_all(packed, 'swath', split_axis=0, concat_axis=0, tiled=True)  4.69 us
    unnamed x14, local copies, waits for them, and re-layouts  3.86 us
  transfers between devices with their start and end apart: 2, of which 1 were waited for; matrix products, arithmetic and copies ran while one was open for 2% of the time, Pallas kernels for 0%

commit v1 on v0

--- a/solution.py
+++ b/solution.py
@@ -20,6 +20,7 @@
 COL_BLOCKS = SWATHS * COLS // BLK_C
 WIDE = SWATHS * COLS + 2 * BLK_C
 PIECE = COLS + BLK_C
+SENT = PIECE + BLK_C
 VMEM_LIMIT = 24 * 1024 * 1024
 
 TAPS = (-0.5, 0.25, 1.0, 0.25, -0.5)
@@ -55,7 +56,18 @@
         out_ref[band, :, CH * COLS :] = jnp.concatenate([first, halo], axis=0).astype(jnp.bfloat16)
 
 
-def norm_kernel(band, recv_ref, sten_ref, out_ref, image_ref, cls_v, cls_s, sem):
+def near_tile(band, near_ref):
+    blocks = ROWS // BLK_R
+    lane = lax.broadcasted_iota(jnp.int32, (16, BLK_C), 1)
+    tile = jnp.zeros((16, BLK_C), jnp.int32)
+    for i in range(4):
+        block = jnp.clip(2 * band - 1 + i, 0, blocks - 1)
+        for k in range(2):
+            tile = jnp.where(lane == 2 * i + k, near_ref[k, block], tile)
+    return tile.astype(jnp.float32)
+
+
+def norm_kernel(band, recv_ref, sten_ref, near_ref, out_ref, image_ref, cls_v, cls_s, sem):
     if band is None:
         band = lax.axis_index("swath")
     before = jnp.maximum(band - 1, 0)
@@ -78,6 +90,7 @@
             image_ref[h, 0:16, lanes] = recv_ref[g, :, h * COLS : (h + 1) * COLS].astype(jnp.float32)
             halo = recv_ref[g, :, CH * COLS :].astype(jnp.float32)[h * 8 : h * 8 + 8]
             image_ref[h, 16:24, lanes] = pltpu.roll(halo, 5, 0)
+    near = near_tile(band, near_ref).astype(jnp.bfloat16)
     copy.wait()
 
     top = jnp.where(band > 0, 1.0, 0.0)
@@ -99,15 +112,13 @@
             below = jnp.zeros((8, BLK_C), jnp.float32)
             for q in range(COLS // BLK_C):
                 block = g * (COLS // BLK_C) + q
-                offsets = [
-                    (cls_s[row, block] * CH + h) * 9 for row in (7, 14, 15, 22)
-                ]
+                kinds = [cls_s[row, block] for row in (7, 14, 15, 22)]
                 total = [jnp.zeros((8, BLK_C), jnp.float32) for _ in range(3)]
                 lanes = slice(q * BLK_C, (q + 1) * BLK_C)
                 for dr in range(3):
                     for dc in range(3):
                         k = 3 * dr + dc
-                        coefs = [sten_ref[offset + k] for offset in offsets]
+                        coefs = [sten_ref[kind, h, k] for kind in kinds]
                         source = shifted[dc][dr]
                         edge = jnp.where(sub < 4, coefs[3] * bottom, coefs[0] * top)
                         total[0] = total[0] + coefs[1] * source[0:8, lanes]
@@ -117,28 +128,32 @@
                 mine = (sub // 2) == q
                 above = jnp.where(mine, pltpu.roll(total[2], (2 * q + 2) % 8, 0), above)
                 below = jnp.where(mine, pltpu.roll(total[2], 2 * q, 0) if q else total[2], below)
-            out_ref[2 * g + h, :, COLS:] = jnp.concatenate([above, below], axis=0).astype(jnp.bfloat16)
+            out_ref[2 * g + h, :, COLS:PIECE] = jnp.concatenate([above, below], axis=0).astype(jnp.bfloat16)
+            out_ref[2 * g + h, :, PIECE:] = near
         return carry
 
     lax.fori_loop(0, SWATHS, step, 0)
 
 
-def pick_kernel(band, near_ref, recv_ref, out_ref):
-    if band is None:
-        band = lax.axis_index("swath")
-    blocks = ROWS // BLK_R
-    first = band * 2
-    rows = (jnp.maximum(first - 1, 0), first, first + 1, jnp.minimum(first + 2, blocks - 1))
+def pick_kernel(recv_ref, out_ref, near_v, near_s, sem):
+    sub = rows_of(16, BLK_C)
+    near = jnp.zeros((16, BLK_C), jnp.float32)
+    for die in range(DIES):
+        near = jnp.where(sub == die, recv_ref[die, :, PIECE:].astype(jnp.float32), near)
+    near_v[...] = near.astype(jnp.int32)
+    copy = pltpu.make_async_copy(near_v, near_s, sem)
+    copy.start()
+    copy.wait()
     main_top = rows_of(16, COLS) < 8
-    edge_top = rows_of(16, BLK_C) < 8
+    edge_top = sub < 8
     for die in range(DIES):
         for k in range(2):
-            up, one, two, down = [near_ref[(die * blocks + row) * 2 + k] for row in rows]
+            up, one, two, down = [near_s[die, 2 * i + k] for i in range(4)]
             out_ref[2 * die + k, :, 0:COLS] = jnp.where(
                 main_top, recv_ref[one, :, 0:COLS], recv_ref[two, :, 0:COLS]
             )
             out_ref[2 * die + k, :, COLS:] = jnp.where(
-                edge_top, recv_ref[up, :, COLS:], recv_ref[down, :, COLS:]
+                edge_top, recv_ref[up, :, COLS:PIECE], recv_ref[down, :, COLS:PIECE]
             )
 
 
@@ -152,7 +167,7 @@
     return jnp.concatenate(tiles, axis=1)
 
 
-def filter_kernel(own_ref, near_ref, out_ref, differ_ref):
+def filter_kernel(own_ref, near_ref, out_ref, differ_ref, done_ref, sems):
     for h in range(CH):
         for k in range(2):
             differ_ref[h, k, :, 0:BLK_C] = jnp.zeros((24, BLK_C), jnp.float32)
@@ -162,7 +177,7 @@
         base = pl.multiple_of(BLK_C + g * COLS, BLK_C)
         for h in range(CH):
             part = 2 * g + h
-            own = own_ref[part].astype(jnp.float32)
+            own = own_ref[part, :, 0:PIECE].astype(jnp.float32)
             for k in range(2):
                 differ = own - near_ref[2 * part + k].astype(jnp.float32)
                 differ_ref[h, k, 0:16, pl.ds(base, COLS)] = differ[:, 0:COLS]
@@ -198,10 +213,13 @@
                 ]
                 lowest = found if lowest is None else [jnp.minimum(a, b) for a, b in zip(lowest, found)]
             for d in range(4):
-                out_ref[d, g, :, h * COLS : (h + 1) * COLS] = lowest[d].astype(jnp.bfloat16)
+                done_ref[g, d, :, h * COLS : (h + 1) * COLS] = lowest[d].astype(jnp.bfloat16)
+        pltpu.make_async_copy(done_ref.at[g], out_ref.at[:, g], sems.at[g]).start()
         return carry
 
     lax.fori_loop(0, SWATHS, step, 0)
+    for g in range(SWATHS):
+        pltpu.make_async_copy(done_ref.at[g], out_ref.at[:, g], sems.at[g]).wait()
 
 
 VMEM = pl.BlockSpec(memory_space=pltpu.VMEM)
@@ -221,11 +239,11 @@
     )(pixels, classes)
 
 
-def norm(recv, stencils, band=None, interpret=False):
+def norm(recv, stencils, near, band=None, interpret=False):
     return pl.pallas_call(
         functools.partial(norm_kernel, band),
-        out_shape=jax.ShapeDtypeStruct((PARTS, BAND, PIECE), jnp.bfloat16),
-        in_specs=[VMEM, SMEM],
+        out_shape=jax.ShapeDtypeStruct((PARTS, BAND, SENT), jnp.bfloat16),
+        in_specs=[VMEM, SMEM, SMEM],
         out_specs=VMEM,
         scratch_shapes=[
             pltpu.VMEM((CH, 24, WIDE), jnp.float32),
@@ -235,18 +253,23 @@
         ],
         compiler_params=PARAMS,
         interpret=interpret,
-    )(recv, stencils)
-
-
-def pick(near, recv, band=None, interpret=False):
+    )(recv, stencils, near)
+
+
+def pick(recv, interpret=False):
     return pl.pallas_call(
-        functools.partial(pick_kernel, band),
+        pick_kernel,
         out_shape=jax.ShapeDtypeStruct((2 * DIES, BAND, PIECE), jnp.bfloat16),
-        in_specs=[SMEM, VMEM],
+        in_specs=[VMEM],
         out_specs=VMEM,
+        scratch_shapes=[
+            pltpu.VMEM((16, BLK_C), jnp.int32),
+            pltpu.SMEM((16, BLK_C), jnp.int32),
+            pltpu.SemaphoreType.DMA,
+        ],
         compiler_params=PARAMS,
         interpret=interpret,
-    )(near, recv)
+    )(recv)
 
 
 def filters(own, near, interpret=False):
@@ -254,20 +277,23 @@
         filter_kernel,
         out_shape=jax.ShapeDtypeStruct((4, SWATHS, BAND, CH * COLS), jnp.bfloat16),
         in_specs=[VMEM, VMEM],
-        out_specs=VMEM,
-        scratch_shapes=[pltpu.VMEM((CH, 2, 24, WIDE), jnp.float32)],
+        out_specs=pl.BlockSpec(memory_space=pl.ANY),
+        scratch_shapes=[
+            pltpu.VMEM((CH, 2, 24, WIDE), jnp.float32),
+            pltpu.VMEM((SWATHS, 4, BAND, CH * COLS), jnp.bfloat16),
+            pltpu.SemaphoreType.DMA((SWATHS,)),
+        ],
         compiler_params=PARAMS,
         interpret=interpret,
     )(own, near)
 
 
 def shards(swath_pixels, stencils, classes, neighbours):
-    near = lax.all_gather(neighbours.reshape(-1), "seg", axis=0, tiled=True)
     packed = pack(swath_pixels[0, 0], classes[0])
     bands = lax.all_to_all(packed, "swath", split_axis=0, concat_axis=0, tiled=True)
-    own = norm(bands, stencils.reshape(-1))
+    own = norm(bands, stencils, neighbours[0].T)
     pieces = lax.all_to_all(own, "seg", split_axis=0, concat_axis=0, tiled=True)
-    picked = pick(near, pieces)
+    picked = pick(pieces)
     references = lax.all_to_all(picked, "seg", split_axis=0, concat_axis=0, tiled=True)
     return filters(own, references)[None]
 

time: 68 us -> 57 us (0.84)
  blocking collectives: 30.1 us -> 45.6 us
  starting transfers between devices: 12.6 us -> 0 us
  waiting for transfers between devices: 8.85 us -> 0 us
  Pallas kernels: 11.2 us -> 8.73 us
  local copies, waits for them, and re-layouts: 4.04 us -> 2.31 us
  between operations: 0.73 us -> 0.03 us
    all_to_all x0 -> x2, blocking collectives: none -> 30.9 us  [the longest x1 17.6 us: shards(): pieces = lax.all_to_all(own, 'seg', split_axis=0, concat_axis=0, tiled=True)]
    unnamed x1 -> x0, blocking collectives: 16.6 us -> none
    all_to_all x2 -> x0, starting transfers between devices: 12.6 us -> none  [the longest x1 7.89 us: shards(): pieces = lax.all_to_all(own, 'seg', split_axis=0, concat_axis=0, tiled=True)]
    all_to_all x2 -> x0, waiting for transfers between devices: 8.85 us -> none  [the longest x1 8.84 us: shards(): lax.all_to_all(packed, 'swath', split_axis=0, concat_axis=0, tiled=True)]
    unnamed x14 -> x8, local copies, waits for them, and re-layouts: 3.86 us -> 2.31 us
    all_to_all x1, blocking collectives: 13.5 us -> 14.8 us  [shards(): lax.all_to_all(picked, 'seg', split_axis=0, concat_axis=0, tiled=True)]
    pallas_call x1, Pallas kernels: 4.82 us -> 3.61 us  [filters(): pl.pallas_call(filter_kernel, out_shape=jax.ShapeDtypeStruct((4, SWATHS,...]
    pallas_call x1, Pallas kernels: 0.81 us -> 0.06 us  [pack(): pl.pallas_call(pack_kernel, out_shape=jax.ShapeDtypeStruct((SWATHS, BAND,...]
  transfers between devices with their start and end apart: 2 -> 0, of which waited for: 1 -> 0; matrix products, arithmetic and copies ran while one was open for 2% -> 0% of each run, Pallas kernels for 0% -> 0%
where the time goes in v1:
time: 57 us; the launch traced here: 56.7 us
  blocking collectives  45.6 us (80%)
  Pallas kernels  8.73 us (15%)
  local copies, waits for them, and re-layouts  2.31 us (4%)
    all_to_all x1, blocking collectives, shards(): pieces = lax.all_to_all(own, 'seg', split_axis=0, concat_axis=0, tiled=True)  17.6 us
    all_to_all x1, blocking collectives, shards(): lax.all_to_all(picked, 'seg', split_axis=0, concat_axis=0, tiled=True)  14.8 us
    all_to_all x1, blocking collectives, shards(): lax.all_to_all(packed, 'swath', split_axis=0, concat_axis=0, tiled=True)  13.3 us
    pallas_call x1, Pallas kernels, norm(): pl.pallas_call(functools.partial(norm_kernel, band), out_shape=jax.ShapeD...  4.26 us
    pallas_call x1, Pallas kernels, filters(): pl.pallas_call(filter_kernel, out_shape=jax.ShapeDtypeStruct((4, SWATHS,...  3.61 us
    unnamed x8, local copies, waits for them, and re-layouts  2.31 us

profile of v1, /device:TPU:0, one launch (start us, length us, event | category | flops | bytes accessed | tf_op | source)
XLA Modules:
  0.0 56.7 jit_solution(10820833712423485088)
XLA Ops:
  0.0 0.0 copy-start.2
  0.0 0.7 %copy-done.2 = s32[1,2,32]{2,1,0:T(2,128)S(1)} copy-done((s32[1,2,32]{2,1,0:T(2,128)S(1)}, s32[1,2,32]{2,1,0:T(2,128)}, u32[]{:S(2)}) %copy-start.2) | copy-done | bytes 280
  0.7 0.0 copy-start
  0.7 0.9 %copy-done = bf16[1,1,128,1024]{3,2,1,0:T(8,128)(2,1)S(1)} copy-done((bf16[1,1,128,1024]{3,2,1,0:T(8,128)(2,1)S(1)}, bf16[1,1,128,1024]{3,2,1,0:T(8,128)(2,1)}, u32[]{:S(2)}) %copy-start) | copy-done | bytes 262168
  1.6 0.1 shard_map.46
  1.7 0.0 copy-start.1
  1.7 13.3 %all_to_all.15.recv_ref = bf16[8,16,1536]{2,1,0:T(8,128)(2,1)S(1)} all-to-all(bf16[8,16,1536]{2,1,0:T(8,128)(2,1)S(1)} %shard_map.46), channel_id=1, replica_groups=mesh['swath'=8,'seg'=16] {'swath'}, dimensions={0} | all-to-all | bytes 786432 | tf_op jit(solution)/shard_map/all_to_all | solution.py:293
  15.0 0.0 copy-start.3
  15.0 0.0 copy-done.1
  15.0 0.7 %copy-done.3 = s32[1,16,2]{1,2,0:T(2,128)S(1)} copy-done((s32[1,16,2]{1,2,0:T(2,128)S(1)}, s32[1,16,2]{1,2,0:T(2,128)}, u32[]{:S(2)}) %copy-start.3) | copy-done | bytes 152
  15.7 4.3 %shard_map.47.own_ref = bf16[16,16,768]{2,1,0:T(8,128)(2,1)S(1)} custom-call(bf16[8,16,1536]{2,1,0:T(8,128)(2,1)S(1)} %all_to_all.15.recv_ref, f32[8,2,9]{2,1,0:T(2,128)S(1)} %copy-done.1, s32[2,16]{1,0:T(2,128)S(1)} %bitcast.8), custom_call_target="tpu_custom_call" | custom-call | tf_op jit(solution)/shard_map/pallas_call | solution.py:243
  19.9 17.6 %all_to_all.16.recv_ref = bf16[16,16,768]{2,1,0:T(8,128)(2,1)S(1)} all-to-all(bf16[16,16,768]{2,1,0:T(8,128)(2,1)S(1)} %shard_map.47.own_ref), channel_id=1, replica_groups=mesh['swath'=8,'seg'=16] {'seg'}, dimensions={0} | all-to-all | bytes 786432 | tf_op jit(solution)/shard_map/all_to_all | solution.py:295
  37.5 0.8 %shard_map.48 = bf16[32,16,640]{2,1,0:T(8,128)(2,1)S(1)} custom-call(bf16[16,16,768]{2,1,0:T(8,128)(2,1)S(1)} %all_to_all.16.recv_ref), custom_call_target="tpu_custom_call" | custom-call | tf_op jit(solution)/shard_map/pallas_call | solution.py:260
  38.3 14.8 %all_to_all.17.near_ref = bf16[32,16,640]{2,1,0:T(8,128)(2,1)S(1)} all-to-all(bf16[32,16,640]{2,1,0:T(8,128)(2,1)S(1)} %shard_map.48), channel_id=1, replica_groups=mesh['swath'=8,'seg'=16] {'seg'}, dimensions={0} | all-to-all | bytes 1310720 | tf_op jit(solution)/shard_map/all_to_all | solution.py:297
  53.1 3.6 %shard_map.49 = bf16[4,8,16,1024]{3,2,1,0:T(8,128)(2,1)} custom-call(bf16[16,16,768]{2,1,0:T(8,128)(2,1)S(1)} %shard_map.47.own_ref, bf16[32,16,640]{2,1,0:T(8,128)(2,1)S(1)} %all_to_all.17.near_ref), custom_call_target="tpu_custom_call" | custom-call | tf_op jit(solution)/shard_map/pallas_call | solution.py:276
Async XLA Ops:
  0.0 0.7 %copy-start.2 = (s32[1,2,32]{2,1,0:T(2,128)S(1)}, s32[1,2,32]{2,1,0:T(2,128)}, u32[]{:S(2)}) copy-start(s32[1,2,32]{2,1,0:T(2,128)} %param.6) | copy-start | bytes 772
  0.7 0.9 %copy-start = (bf16[1,1,128,1024]{3,2,1,0:T(8,128)(2,1)S(1)}, bf16[1,1,128,1024]{3,2,1,0:T(8,128)(2,1)}, u32[]{:S(2)}) copy-start(bf16[1,1,128,1024]{3,2,1,0:T(8,128)(2,1)} %param.4) | copy-start | bytes 786436
  1.7 13.3 %copy-start.1 = (f32[8,2,9]{2,1,0:T(2,128)S(1)}, f32[8,2,9]{2,1,0:T(2,128)}, u32[]{:S(2)}) copy-start(f32[8,2,9]{2,1,0:T(2,128)} %sten_ref.1) | copy-start | bytes 1732
  15.0 0.7 %copy-start.3 = (s32[1,16,2]{1,2,0:T(2,128)S(1)}, s32[1,16,2]{1,2,0:T(2,128)}, u32[]{:S(2)}) copy-start(s32[1,16,2]{1,2,0:T(2,128)} %param.7) | copy-start | bytes 388

commit v2 on v1

v2 whole, which is shorter than its diff:
```python
import functools

import jax
import jax.numpy as jnp
from jax import lax
from jax.experimental import pallas as pl
from jax.experimental.pallas import tpu as pltpu
from jax.sharding import PartitionSpec as P

CH = 2
BLK_R = 8
BLK_C = 128
NCLASS = 8
SWATHS = 8
DIES = 16
ROWS = 128
COLS = 512
BAND = 16
PARTS = 16
COL_BLOCKS = SWATHS * COLS // BLK_C
QUADS = COLS // BLK_C
TILES = SWATHS * QUADS + 2
PIECE = COLS + BLK_C
SENT = PIECE + BLK_C
VMEM_LIMIT = 32 * 1024 * 1024

TAPS = (-0.5, 0.25, 1.0, 0.25, -0.5)
DIRECTIONS = ((0, 1), (1, 0), (1, 1), (1, -1))


def rows_of(count, width):
    return lax.broadcasted_iota(jnp.int32, (count, width), 0)


def pack_kernel(band, pix_ref, cls_ref, ids_ref, out_ref, near_ref, row_ref):
    if band is None:
        band = lax.axis_index("swath")
    row_ref[...] = jnp.zeros_like(row_ref)
    row_ref[0:2, 0 : ROWS // BLK_R] = ids_ref[...].astype(jnp.float32)
    ids = pltpu.roll(row_ref[:, 0:BLK_C], (BLK_C + 1 - 2 * band) % BLK_C, 1)
    near_ref[...] = jnp.concatenate([ids, jnp.zeros_like(ids)], axis=0).astype(jnp.bfloat16)

    row_ref[...] = jnp.zeros_like(row_ref)
    row_ref[6:8, 0:COL_BLOCKS] = cls_ref[...].astype(jnp.float32)
    own_classes = row_ref[...]
    sub = rows_of(8, COLS)
    for piece in range(SWATHS):
        start = piece * BAND
        out_ref[piece, :, 0 : CH * COLS] = pix_ref[start : start + BAND, :]
        halves = []
        for h in range(CH):
            lanes = slice(h * COLS, (h + 1) * COLS)
            above = jnp.zeros((8, COLS), jnp.float32)
            below = jnp.zeros((8, COLS), jnp.float32)
            if piece > 0:
                above = pltpu.roll(pix_ref[start - BAND : start, lanes].astype(jnp.float32)[8:16], 3, 0)
            if piece < SWATHS - 1:
                below = pltpu.roll(pix_ref[start + BAND : start + 2 * BAND, lanes].astype(jnp.float32)[0:8], 3, 0)
            halves.append(jnp.where(sub < 3, above, jnp.where(sub < 6, below, own_classes)))
        out_ref[piece, :, CH * COLS :] = jnp.concatenate(halves, axis=0).astype(jnp.bfloat16)


def window_of(ref, h, g):
    return jnp.concatenate([ref[h, QUADS * g + q, 0:24] for q in range(QUADS + 2)], axis=1)


def store_shifted(ref, h, g, window, shift):
    width = (QUADS + 2) * BLK_C
    moved = pltpu.roll(window, (-shift) % width, 1)
    for q in range(QUADS):
        value = moved[:, (q + 1) * BLK_C : (q + 2) * BLK_C]
        ref[h, QUADS * g + q + 1, 0:24] = value
        ref[h, QUADS * g + q + 1, 24:32] = value[0:8]


def store_ring(ref, h, tile, rows, halo):
    ref[h, tile, 0:8] = halo
    ref[h, tile, 8:24] = rows
    ref[h, tile, 24:32] = halo


def norm_kernel(
    band, recv_ref, sten_ref, near_ref, out_ref, left_ref, image_ref, right_ref, table_ref, cls_v, cls_s, sem
):
    if band is None:
        band = lax.axis_index("swath")
    before = jnp.maximum(band - 1, 0)
    after = jnp.minimum(band + 1, SWATHS - 1)

    def class_rows(source):
        return recv_ref[source, :, CH * COLS : CH * COLS + BLK_C].astype(jnp.float32)[0:8].astype(jnp.int32)

    cls_v[0:8] = class_rows(before)
    cls_v[8:16] = class_rows(band)
    cls_v[16:24] = class_rows(after)
    copy = pltpu.make_async_copy(cls_v, cls_s, sem)
    copy.start()

    for k in range(CH * 9):
        table_ref[NCLASS, k] = jnp.zeros((8, BLK_C), jnp.float32)
    for kind in range(NCLASS):
        for h in range(CH):
            row = sten_ref[kind, h : h + 1, :]
            for k in range(9):
                table_ref[kind, CH * k + h] = jnp.broadcast_to(row[:, k : k + 1], (8, BLK_C))

    near = near_ref[...]
    sub = rows_of(8, BLK_C)
    for h in range(CH):
        image_ref[h, 0] = jnp.zeros((32, BLK_C), jnp.float32)
        image_ref[h, TILES - 1] = jnp.zeros((32, BLK_C), jnp.float32)
    for g in range(SWATHS):
        for h in range(CH):
            halo = pltpu.roll(recv_ref[g, :, CH * COLS :].astype(jnp.float32)[h * 8 : h * 8 + 8], 5, 0)
            for q in range(QUADS):
                lanes = slice(h * COLS + q * BLK_C, h * COLS + (q + 1) * BLK_C)
                rows = recv_ref[g, :, lanes].astype(jnp.float32)
                store_ring(image_ref, h, QUADS * g + q + 1, rows, halo[:, q * BLK_C : (q + 1) * BLK_C])

    def shift(g):
        for h in range(CH):
            window = window_of(image_ref, h, g)
            store_shifted(left_ref, h, g, window, -1)
            store_shifted(right_ref, h, g, window, 1)

    def step(g):
        for h in range(CH):
            above = jnp.zeros((8, BLK_C), jnp.float32)
            below = jnp.zeros((8, BLK_C), jnp.float32)
            for q in range(QUADS):
                block = g * QUADS + q
                tile = block + 1
                kinds = [cls_s[row, block] for row in (7, 14, 15, 22)]
                kinds[0] = jnp.where(band > 0, kinds[0], NCLASS)
                kinds[3] = jnp.where(band < SWATHS - 1, kinds[3], NCLASS)
                total = [None] * 3
                for dr in range(3):
                    for dc, source in enumerate((left_ref, image_ref, right_ref)):
                        coefs = [table_ref[kind, CH * (3 * dr + dc) + h] for kind in kinds]
                        rows = source[h, tile, pl.ds(7 + dr, BAND)]
                        halo = source[h, tile, pl.ds((23, 0, 1)[dr], 8)]
                        terms = [
                            coefs[1] * rows[0:8],
                            coefs[2] * rows[8:16],
                            jnp.where(sub < 4, coefs[3], coefs[0]) * halo,
                        ]
                        total = [t if s is None else s + t for s, t in zip(total, terms)]
                lanes = slice(q * BLK_C, (q + 1) * BLK_C)
                out_ref[2 * g + h, :, lanes] = jnp.concatenate(total[:2], axis=0).astype(jnp.bfloat16)
                mine = (sub // 2) == q
                above = jnp.where(mine, pltpu.roll(total[2], (2 * q + 2) % 8, 0) if q != 3 else total[2], above)
                below = jnp.where(mine, pltpu.roll(total[2], 2 * q, 0) if q else total[2], below)
            out_ref[2 * g + h, :, COLS:PIECE] = jnp.concatenate([above, below], axis=0).astype(jnp.bfloat16)
            out_ref[2 * g + h, :, PIECE:] = near

    shift(0)
    shift(1)
    copy.wait()
    for g in range(SWATHS):
        if g + 2 < SWATHS:
            shift(g + 2)
        step(g)


def pick_kernel(recv_ref, out_ref, near_v, near_s, sem):
    sub = rows_of(2 * DIES, BLK_C)
    for part in range(DIES // 4):
        ids = jnp.zeros((8, BLK_C), jnp.float32)
        for i in range(4):
            rows = recv_ref[4 * part + i, :, PIECE:].astype(jnp.float32)[0:8]
            ids = jnp.where(sub[0:8] // 2 == i, pltpu.roll(rows, 2 * i, 0) if i else rows, ids)
        near_v[8 * part : 8 * part + 8] = ids.astype(jnp.int32)
    copy = pltpu.make_async_copy(near_v, near_s, sem)
    copy.start()
    copy.wait()
    main_top = rows_of(16, COLS) < 8
    edge_top = sub[0:16] < 8
    for die in range(DIES):
        for k in range(2):
            up, one, two, down = [near_s[2 * die + k, i] for i in range(4)]
            out_ref[2 * die + k, :, 0:COLS] = jnp.where(
                main_top, recv_ref[one, :, 0:COLS], recv_ref[two, :, 0:COLS]
            )
            out_ref[2 * die + k, :, COLS:] = jnp.where(
                edge_top, recv_ref[up, :, COLS:PIECE], recv_ref[down, :, COLS:PIECE]
            )


def filter_kernel(own_ref, near_ref, out_ref, *scratch):
    done_ref, sems = scratch[-2:]
    images = [dict(zip(("full", 1, 2, (1, -1), (1, 1), (2, -2), (2, 2)), scratch[7 * k : 7 * k + 7])) for k in range(2)]
    low = rows_of(8, BLK_C) < 4
    for k in range(2):
        for scale in (1, 2):
            for h in range(CH):
                images[k][scale][h, 0] = jnp.zeros((32, BLK_C), jnp.float32)
                images[k][scale][h, TILES - 1] = jnp.zeros((32, BLK_C), jnp.float32)

    def fill(g):
        for h in range(CH):
            part = 2 * g + h
            own = own_ref[part, :, 0:PIECE].astype(jnp.float32)
            for k in range(2):
                differ = own - near_ref[2 * part + k].astype(jnp.float32)
                edge = differ[:, COLS:]
                for q in range(QUADS):
                    tile = QUADS * g + q + 1
                    up, down = (6 - 2 * q) % 8, (8 - 2 * q) % 8
                    above = pltpu.roll(edge[0:8], up, 0) if up else edge[0:8]
                    below = pltpu.roll(edge[8:16], down, 0) if down else edge[8:16]
                    halo = jnp.where(low, below, above)
                    rows = differ[:, q * BLK_C : (q + 1) * BLK_C]
                    images[k]["full"][h, tile] = rows
                    store_ring(images[k][1], h, tile, 0.25 * rows, 0.25 * halo)
                    store_ring(images[k][2], h, tile, -0.5 * rows, -0.5 * halo)

    def shift(g):
        for h in range(CH):
            for k in range(2):
                for scale in (1, 2):
                    window = window_of(images[k][scale], h, g)
                    for sign in (-1, 1):
                        store_shifted(images[k][scale, sign * scale], h, g, window, sign * scale)

    def step(g):
        for h in range(CH):
            for q in range(QUADS):
                tile = QUADS * g + q + 1
                lowest = None
                for k in range(2):
                    middle = images[k]["full"][h, tile]
                    found = []
                    for a, b in DIRECTIONS:
                        terms = []
                        for t in (-2, -1, 1, 2):
                            source = images[k][abs(t), b * t] if b else images[k][abs(t)]
                            terms.append(source[h, tile, pl.ds(8 + a * t, BAND)])
                        found.append((middle + (terms[1] + terms[2])) + (terms[0] + terms[3]))
                    lowest = found if lowest is None else [jnp.minimum(a, b) for a, b in zip(lowest, found)]
                lanes = slice(h * COLS + q * BLK_C, h * COLS + (q + 1) * BLK_C)
                for d in range(4):
                    done_ref[g, d, :, lanes] = lowest[d].astype(jnp.bfloat16)

    def send(g):
        return pltpu.make_async_copy(done_ref.at[g], out_ref.at[:, g], sems.at[g])

    fill(0)
    fill(1)
    shift(0)
    for g in range(SWATHS):
        if g + 2 < SWATHS:
            fill(g + 2)
        if g + 1 < SWATHS:
            shift(g + 1)
        step(g)
        send(g).start()
    for g in range(SWATHS):
        send(g).wait()


VMEM = pl.BlockSpec(memory_space=pltpu.VMEM)
PARAMS = pltpu.CompilerParams(vmem_limit_bytes=VMEM_LIMIT)


def pack(pixels, classes, near, band=None, interpret=False):
    return pl.pallas_call(
        functools.partial(pack_kernel, band),
        out_shape=(
            jax.ShapeDtypeStruct((SWATHS, BAND, 3 * COLS), jnp.bfloat16),
            jax.ShapeDtypeStruct((16, BLK_C), jnp.bfloat16),
        ),
        in_specs=[VMEM] * 3,
        out_specs=(VMEM,) * 2,
        scratch_shapes=[pltpu.VMEM((8, COLS), jnp.float32)],
        compiler_params=PARAMS,
        interpret=interpret,
    )(pixels, classes, near)


def norm(recv, stencils, near, band=None, interpret=False):
    image = pltpu.VMEM((CH, TILES, 32, BLK_C), jnp.float32)
    return pl.pallas_call(
        functools.partial(norm_kernel, band),
        out_shape=jax.ShapeDtypeStruct((PARTS, BAND, SENT), jnp.bfloat16),
        in_specs=[VMEM, VMEM, VMEM],
        out_specs=VMEM,
        scratch_shapes=[
            image,
            image,
            image,
            pltpu.VMEM((NCLASS + 1, CH * 9, 8, BLK_C), jnp.float32),
            pltpu.VMEM((24, BLK_C), jnp.int32),
            pltpu.SMEM((24, BLK_C), jnp.int32),
            pltpu.SemaphoreType.DMA,
        ],
        compiler_params=PARAMS,
        interpret=interpret,
    )(recv, stencils, near)


def pick(recv, interpret=False):
    return pl.pallas_call(
        pick_kernel,
        out_shape=jax.ShapeDtypeStruct((2 * DIES, BAND, PIECE), jnp.bfloat16),
        in_specs=[VMEM],
        out_specs=VMEM,
        scratch_shapes=[
            pltpu.VMEM((2 * DIES, BLK_C), jnp.int32),
            pltpu.SMEM((2 * DIES, BLK_C), jnp.int32),
            pltpu.SemaphoreType.DMA,
        ],
        compiler_params=PARAMS,
        interpret=interpret,
    )(recv)


def filters(own, near, interpret=False):
    full = pltpu.VMEM((CH, TILES, BAND, BLK_C), jnp.float32)
    image = pltpu.VMEM((CH, TILES, 32, BLK_C), jnp.float32)
    return pl.pallas_call(
        filter_kernel,
        out_shape=jax.ShapeDtypeStruct((4, SWATHS, BAND, CH * COLS), jnp.bfloat16),
        in_specs=[VMEM, VMEM],
        out_specs=pl.BlockSpec(memory_space=pl.ANY),
        scratch_shapes=[
            *([full] + [image] * 6) * 2,
            pltpu.VMEM((SWATHS, 4, BAND, CH * COLS), jnp.bfloat16),
            pltpu.SemaphoreType.DMA((SWATHS,)),
        ],
        compiler_params=PARAMS,
        interpret=interpret,
    )(own, near)


def shards(swath_pixels, stencils, classes, neighbours):
    packed, near = pack(swath_pixels[0, 0], classes[0], neighbours[0].T)
    bands = lax.all_to_all(packed, "swath", split_axis=0, concat_axis=0, tiled=True)
    own = norm(bands, stencils, near)
    pieces = lax.all_to_all(own, "seg", split_axis=0, concat_axis=0, tiled=True)
    picked = pick(pieces)
    references = lax.all_to_all(picked, "seg", split_axis=0, concat_axis=0, tiled=True)
    return filters(own, references)[None]


def solution(mesh):
    return jax.shard_map(
        shards,
        mesh=mesh,
        in_specs=(
            P("swath", "seg", None, None),
            P(),
            P("seg", "swath", None),
            P("seg", None, None),
        ),
        out_specs=P("seg", None, None, "swath", None),
        check_vma=False,
    )
```

time: 57 us -> 54.3 us (0.953)
  Pallas kernels: 8.73 us -> 6.53 us
  local copies, waits for them, and re-layouts: 2.31 us -> 1.65 us
    pallas_call x1, Pallas kernels: 4.26 us -> 2.33 us  [norm(): pl.pallas_call(functools.partial(norm_kernel, band), out_shape=jax.ShapeD...]
    unnamed x8, local copies, waits for them, and re-layouts: 2.31 us -> 1.65 us
where the time goes in v2:
time: 54.3 us; the launch traced here: 54.1 us
  blocking collectives  45.9 us (85%)
  Pallas kernels  6.53 us (12%)
  local copies, waits for them, and re-layouts  1.65 us (3%)
    all_to_all x1, blocking collectives, shards(): pieces = lax.all_to_all(own, 'seg', split_axis=0, concat_axis=0, tiled=True)  17.6 us
    all_to_all x1, blocking collectives, shards(): lax.all_to_all(picked, 'seg', split_axis=0, concat_axis=0, tiled=True)  14.8 us
    all_to_all x1, blocking collectives, shards(): lax.all_to_all(packed, 'swath', split_axis=0, concat_axis=0, tiled=True)  13.4 us
    pallas_call x1, Pallas kernels, filters(): pl.pallas_call(filter_kernel, out_shape=jax.ShapeDtypeStruct((4, SWATHS,...  3.17 us
    pallas_call x1, Pallas kernels, norm(): pl.pallas_call(functools.partial(norm_kernel, band), out_shape=jax.ShapeD...  2.33 us
    unnamed x8, local copies, waits for them, and re-layouts  1.65 us

profile of v2, /device:TPU:0, one launch (start us, length us, event | category | flops | bytes accessed | tf_op | source)
XLA Modules:
  0.0 54.1 jit_solution(303981521547539440)
XLA Ops:
  0.0 0.0 copy-start.3
  0.0 0.0 copy-start.2
  0.0 0.7 %copy-done.3 = s32[1,16,2]{1,2,0:T(2,128)S(1)} copy-done((s32[1,16,2]{1,2,0:T(2,128)S(1)}, s32[1,16,2]{1,2,0:T(2,128)}, u32[]{:S(2)}) %copy-start.3) | copy-done | bytes 152
  0.7 0.0 copy-done.2
  0.7 0.0 copy-start
  0.7 0.9 %copy-done = bf16[1,1,128,1024]{3,2,1,0:T(8,128)(2,1)S(1)} copy-done((bf16[1,1,128,1024]{3,2,1,0:T(8,128)(2,1)S(1)}, bf16[1,1,128,1024]{3,2,1,0:T(8,128)(2,1)}, u32[]{:S(2)}) %copy-start) | copy-done | bytes 262168
  1.6 0.1 shard_map.46
  1.7 0.0 copy-start.1
  1.7 13.4 %all_to_all.15.recv_ref = bf16[8,16,1536]{2,1,0:T(8,128)(2,1)S(1)} all-to-all(bf16[8,16,1536]{2,1,0:T(8,128)(2,1)S(1)} %get-tuple-element.7), channel_id=1, replica_groups=mesh['swath'=8,'seg'=16] {'swath'}, dimensions={0} | all-to-all | bytes 786432 | tf_op jit(solution)/shard_map/all_to_all | solution.py:337
  15.2 0.0 copy-done.1
  15.2 2.3 %shard_map.47.own_ref = bf16[16,16,768]{2,1,0:T(8,128)(2,1)S(1)} custom-call(bf16[8,16,1536]{2,1,0:T(8,128)(2,1)S(1)} %all_to_all.15.recv_ref, f32[8,2,9]{2,1,0:T(2,128)S(1)} %copy-done.1, bf16[16,128]{1,0:T(8,128)(2,1)S(1)} %get-tuple-element.8.near_ref), custom_call_target="tpu_custom_call" | custom-call | tf_op jit(solution)/shard_map/pallas_call | solution.py:282
  17.5 17.6 %all_to_all.16.recv_ref = bf16[16,16,768]{2,1,0:T(8,128)(2,1)S(1)} all-to-all(bf16[16,16,768]{2,1,0:T(8,128)(2,1)S(1)} %shard_map.47.own_ref), channel_id=1, replica_groups=mesh['swath'=8,'seg'=16] {'seg'}, dimensions={0} | all-to-all | bytes 786432 | tf_op jit(solution)/shard_map/all_to_all | solution.py:339
  35.1 0.9 %shard_map.48 = bf16[32,16,640]{2,1,0:T(8,128)(2,1)S(1)} custom-call(bf16[16,16,768]{2,1,0:T(8,128)(2,1)S(1)} %all_to_all.16.recv_ref), custom_call_target="tpu_custom_call" | custom-call | tf_op jit(solution)/shard_map/pallas_call | solution.py:302
  36.1 14.8 %all_to_all.17.near_ref = bf16[32,16,640]{2,1,0:T(8,128)(2,1)S(1)} all-to-all(bf16[32,16,640]{2,1,0:T(8,128)(2,1)S(1)} %shard_map.48), channel_id=1, replica_groups=mesh['swath'=8,'seg'=16] {'seg'}, dimensions={0} | all-to-all | bytes 1310720 | tf_op jit(solution)/shard_map/all_to_all | solution.py:341
  50.9 3.2 %shard_map.49 = bf16[4,8,16,1024]{3,2,1,0:T(8,128)(2,1)} custom-call(bf16[16,16,768]{2,1,0:T(8,128)(2,1)S(1)} %shard_map.47.own_ref, bf16[32,16,640]{2,1,0:T(8,128)(2,1)S(1)} %all_to_all.17.near_ref), custom_call_target="tpu_custom_call" | custom-call | tf_op jit(solution)/shard_map/pallas_call | solution.py:320
Async XLA Ops:
  0.0 0.7 %copy-start.3 = (s32[1,16,2]{1,2,0:T(2,128)S(1)}, s32[1,16,2]{1,2,0:T(2,128)}, u32[]{:S(2)}) copy-start(s32[1,16,2]{1,2,0:T(2,128)} %param.7) | copy-start | bytes 388
  0.0 0.7 %copy-start.2 = (s32[1,2,32]{2,1,0:T(2,128)S(1)}, s32[1,2,32]{2,1,0:T(2,128)}, u32[]{:S(2)}) copy-start(s32[1,2,32]{2,1,0:T(2,128)} %param.6) | copy-start | bytes 772
  0.7 0.9 %copy-start = (bf16[1,1,128,1024]{3,2,1,0:T(8,128)(2,1)S(1)}, bf16[1,1,128,1024]{3,2,1,0:T(8,128)(2,1)}, u32[]{:S(2)}) copy-start(bf16[1,1,128,1024]{3,2,1,0:T(8,128)(2,1)} %param.4) | copy-start | bytes 786436
  1.7 13.4 %copy-start.1 = (f32[8,2,9]{2,1,0:T(2,128)S(1)}, f32[8,2,9]{2,1,0:T(2,128)}, u32[]{:S(2)}) copy-start(f32[8,2,9]{2,1,0:T(2,128)} %sten_ref.1) | copy-start | bytes 1732

commit v3 on v2

--- a/solution.py
+++ b/solution.py
@@ -60,17 +60,27 @@
         out_ref[piece, :, CH * COLS :] = jnp.concatenate(halves, axis=0).astype(jnp.bfloat16)
 
 
-def window_of(ref, h, g):
-    return jnp.concatenate([ref[h, QUADS * g + q, 0:24] for q in range(QUADS + 2)], axis=1)
-
-
-def store_shifted(ref, h, g, window, shift):
-    width = (QUADS + 2) * BLK_C
-    moved = pltpu.roll(window, (-shift) % width, 1)
-    for q in range(QUADS):
-        value = moved[:, (q + 1) * BLK_C : (q + 2) * BLK_C]
-        ref[h, QUADS * g + q + 1, 0:24] = value
-        ref[h, QUADS * g + q + 1, 24:32] = value[0:8]
+def shifter(ref):
+    rotated = {}
+    lane = lax.broadcasted_iota(jnp.int32, (24, BLK_C), 1)
+
+    def turn(h, tile, shift):
+        if tile == 0 or tile == TILES - 1:
+            return jnp.zeros((24, BLK_C), jnp.float32)
+        if (h, tile, shift) not in rotated:
+            rotated[h, tile, shift] = pltpu.roll(ref[h, tile, 0:24], (-shift) % BLK_C, 1)
+        return rotated[h, tile, shift]
+
+    def store(target, h, g, shift):
+        for tile in range(QUADS * g + 1, QUADS * g + QUADS + 1):
+            if shift > 0:
+                value = jnp.where(lane < BLK_C - shift, turn(h, tile, shift), turn(h, tile + 1, shift))
+            else:
+                value = jnp.where(lane < -shift, turn(h, tile - 1, shift), turn(h, tile, shift))
+            target[h, tile, 0:24] = value
+            target[h, tile, 24:32] = value[0:8]
+
+    return store
 
 
 def store_ring(ref, h, tile, rows, halo):
@@ -80,7 +90,7 @@
 
 
 def norm_kernel(
-    band, recv_ref, sten_ref, near_ref, out_ref, left_ref, image_ref, right_ref, table_ref, cls_v, cls_s, sem
+    band, recv_ref, sten_ref, near_ref, out_ref, left_ref, image_ref, right_ref, table_ref
 ):
     if band is None:
         band = lax.axis_index("swath")
@@ -90,11 +100,12 @@
     def class_rows(source):
         return recv_ref[source, :, CH * COLS : CH * COLS + BLK_C].astype(jnp.float32)[0:8].astype(jnp.int32)
 
-    cls_v[0:8] = class_rows(before)
-    cls_v[8:16] = class_rows(band)
-    cls_v[16:24] = class_rows(after)
-    copy = pltpu.make_async_copy(cls_v, cls_s, sem)
-    copy.start()
+    sub = rows_of(8, BLK_C)
+    mine = class_rows(band)
+    above = jnp.where(band > 0, class_rows(before), NCLASS)
+    below = jnp.where(band < SWATHS - 1, class_rows(after), NCLASS)
+    above, below = pltpu.roll(above, 1, 0), pltpu.roll(below, 2, 0)
+    code = above * 4096 + pltpu.roll(mine, 2, 0) * 256 + pltpu.roll(mine, 1, 0) * 16 + below
 
     for k in range(CH * 9):
         table_ref[NCLASS, k] = jnp.zeros((8, BLK_C), jnp.float32)
@@ -105,10 +116,7 @@
                 table_ref[kind, CH * k + h] = jnp.broadcast_to(row[:, k : k + 1], (8, BLK_C))
 
     near = near_ref[...]
-    sub = rows_of(8, BLK_C)
-    for h in range(CH):
-        image_ref[h, 0] = jnp.zeros((32, BLK_C), jnp.float32)
-        image_ref[h, TILES - 1] = jnp.zeros((32, BLK_C), jnp.float32)
+    shifted = shifter(image_ref)
     for g in range(SWATHS):
         for h in range(CH):
             halo = pltpu.roll(recv_ref[g, :, CH * COLS :].astype(jnp.float32)[h * 8 : h * 8 + 8], 5, 0)
@@ -119,9 +127,8 @@
 
     def shift(g):
         for h in range(CH):
-            window = window_of(image_ref, h, g)
-            store_shifted(left_ref, h, g, window, -1)
-            store_shifted(right_ref, h, g, window, 1)
+            shifted(left_ref, h, g, -1)
+            shifted(right_ref, h, g, 1)
 
     def step(g):
         for h in range(CH):
@@ -130,9 +137,7 @@
             for q in range(QUADS):
                 block = g * QUADS + q
                 tile = block + 1
-                kinds = [cls_s[row, block] for row in (7, 14, 15, 22)]
-                kinds[0] = jnp.where(band > 0, kinds[0], NCLASS)
-                kinds[3] = jnp.where(band < SWATHS - 1, kinds[3], NCLASS)
+                kinds = [(codes[block] >> bits) & 15 for bits in (12, 8, 4, 0)]
                 total = [None] * 3
                 for dr in range(3):
                     for dc, source in enumerate((left_ref, image_ref, right_ref)):
@@ -153,31 +158,34 @@
             out_ref[2 * g + h, :, COLS:PIECE] = jnp.concatenate([above, below], axis=0).astype(jnp.bfloat16)
             out_ref[2 * g + h, :, PIECE:] = near
 
-    shift(0)
-    shift(1)
-    copy.wait()
+    lead = 2
+    codes = [code[0, block] for block in range(COL_BLOCKS)]
+    for g in range(lead):
+        shift(g)
     for g in range(SWATHS):
-        if g + 2 < SWATHS:
-            shift(g + 2)
+        if g + lead < SWATHS:
+            shift(g + lead)
         step(g)
 
 
-def pick_kernel(recv_ref, out_ref, near_v, near_s, sem):
-    sub = rows_of(2 * DIES, BLK_C)
+def pick_kernel(recv_ref, out_ref):
+    sub = rows_of(16, BLK_C)
+    codes = []
     for part in range(DIES // 4):
         ids = jnp.zeros((8, BLK_C), jnp.float32)
         for i in range(4):
             rows = recv_ref[4 * part + i, :, PIECE:].astype(jnp.float32)[0:8]
             ids = jnp.where(sub[0:8] // 2 == i, pltpu.roll(rows, 2 * i, 0) if i else rows, ids)
-        near_v[8 * part : 8 * part + 8] = ids.astype(jnp.int32)
-    copy = pltpu.make_async_copy(near_v, near_s, sem)
-    copy.start()
-    copy.wait()
+        code = ids * 4096.0
+        for i, scale in ((1, 256.0), (2, 16.0), (3, 1.0)):
+            code = code + scale * pltpu.roll(ids, BLK_C - i, 1)
+        codes.append(code.astype(jnp.int32))
     main_top = rows_of(16, COLS) < 8
-    edge_top = sub[0:16] < 8
+    edge_top = sub < 8
     for die in range(DIES):
         for k in range(2):
-            up, one, two, down = [near_s[2 * die + k, i] for i in range(4)]
+            code = codes[die // 4][2 * (die % 4) + k, 0]
+            up, one, two, down = [(code >> bits) & 15 for bits in (12, 8, 4, 0)]
             out_ref[2 * die + k, :, 0:COLS] = jnp.where(
                 main_top, recv_ref[one, :, 0:COLS], recv_ref[two, :, 0:COLS]
             )
@@ -190,11 +198,7 @@
     done_ref, sems = scratch[-2:]
     images = [dict(zip(("full", 1, 2, (1, -1), (1, 1), (2, -2), (2, 2)), scratch[7 * k : 7 * k + 7])) for k in range(2)]
     low = rows_of(8, BLK_C) < 4
-    for k in range(2):
-        for scale in (1, 2):
-            for h in range(CH):
-                images[k][scale][h, 0] = jnp.zeros((32, BLK_C), jnp.float32)
-                images[k][scale][h, TILES - 1] = jnp.zeros((32, BLK_C), jnp.float32)
+    shifted = [{scale: shifter(images[k][scale]) for scale in (1, 2)} for k in range(2)]
 
     def fill(g):
         for h in range(CH):
@@ -218,9 +222,8 @@
         for h in range(CH):
             for k in range(2):
                 for scale in (1, 2):
-                    window = window_of(images[k][scale], h, g)
                     for sign in (-1, 1):
-                        store_shifted(images[k][scale, sign * scale], h, g, window, sign * scale)
+                        shifted[k][scale](images[k][scale, sign * scale], h, g, sign * scale)
 
     def step(g):
         for h in range(CH):
@@ -289,9 +292,6 @@
             image,
             image,
             pltpu.VMEM((NCLASS + 1, CH * 9, 8, BLK_C), jnp.float32),
-            pltpu.VMEM((24, BLK_C), jnp.int32),
-            pltpu.SMEM((24, BLK_C), jnp.int32),
-            pltpu.SemaphoreType.DMA,
         ],
         compiler_params=PARAMS,
         interpret=interpret,
@@ -304,11 +304,6 @@
         out_shape=jax.ShapeDtypeStruct((2 * DIES, BAND, PIECE), jnp.bfloat16),
         in_specs=[VMEM],
         out_specs=VMEM,
-        scratch_shapes=[
-            pltpu.VMEM((2 * DIES, BLK_C), jnp.int32),
-            pltpu.SMEM((2 * DIES, BLK_C), jnp.int32),
-            pltpu.SemaphoreType.DMA,
-        ],
         compiler_params=PARAMS,
         interpret=interpret,
     )(recv)

time: 54.3 us -> 52.5 us (0.967)
  Pallas kernels: 6.53 us -> 4.75 us
    pallas_call x1, Pallas kernels: 2.33 us -> 1.59 us  [norm(): pl.pallas_call(functools.partial(norm_kernel, band), out_shape=jax.ShapeD...]
    pallas_call x1, Pallas kernels: 0.94 us -> 0.26 us  [pick(): pl.pallas_call(pick_kernel, out_shape=jax.ShapeDtypeStruct((2 * DIES, BAN...]
where the time goes in v3:
time: 52.5 us; the launch traced here: 52.2 us
  blocking collectives  45.8 us (87%)
  Pallas kernels  4.75 us (9%)
  local copies, waits for them, and re-layouts  1.65 us (3%)
    all_to_all x1, blocking collectives, shards(): pieces = lax.all_to_all(own, 'seg', split_axis=0, concat_axis=0, tiled=True)  17.6 us
    all_to_all x1, blocking collectives, shards(): lax.all_to_all(picked, 'seg', split_axis=0, concat_axis=0, tiled=True)  14.8 us
    all_to_all x1, blocking collectives, shards(): lax.all_to_all(packed, 'swath', split_axis=0, concat_axis=0, tiled=True)  13.4 us
    pallas_call x1, Pallas kernels, filters(): pl.pallas_call(filter_kernel, out_shape=jax.ShapeDtypeStruct((4, SWATHS,...  2.81 us
    unnamed x8, local copies, waits for them, and re-layouts  1.65 us
    pallas_call x1, Pallas kernels, norm(): pl.pallas_call(functools.partial(norm_kernel, band), out_shape=jax.ShapeD...  1.59 us

profile of v3, /device:TPU:0, one launch (start us, length us, event | category | flops | bytes accessed | tf_op | source)
XLA Modules:
  0.0 52.2 jit_solution(11164244994104395915)
XLA Ops:
  0.0 0.0 copy-start.3
  0.0 0.0 copy-start.2
  0.0 0.7 %copy-done.3 = s32[1,16,2]{1,2,0:T(2,128)S(1)} copy-done((s32[1,16,2]{1,2,0:T(2,128)S(1)}, s32[1,16,2]{1,2,0:T(2,128)}, u32[]{:S(2)}) %copy-start.3) | copy-done | bytes 152
  0.7 0.0 copy-done.2
  0.7 0.0 copy-start
  0.7 0.9 %copy-done = bf16[1,1,128,1024]{3,2,1,0:T(8,128)(2,1)S(1)} copy-done((bf16[1,1,128,1024]{3,2,1,0:T(8,128)(2,1)S(1)}, bf16[1,1,128,1024]{3,2,1,0:T(8,128)(2,1)}, u32[]{:S(2)}) %copy-start) | copy-done | bytes 262168
  1.6 0.1 shard_map.46
  1.7 0.0 copy-start.1
  1.7 13.4 %all_to_all.15.recv_ref = bf16[8,16,1536]{2,1,0:T(8,128)(2,1)S(1)} all-to-all(bf16[8,16,1536]{2,1,0:T(8,128)(2,1)S(1)} %get-tuple-element.7), channel_id=1, replica_groups=mesh['swath'=8,'seg'=16] {'swath'}, dimensions={0} | all-to-all | bytes 786432 | tf_op jit(solution)/shard_map/all_to_all | solution.py:332
  15.2 0.0 copy-done.1
  15.2 1.6 %shard_map.47.own_ref = bf16[16,16,768]{2,1,0:T(8,128)(2,1)S(1)} custom-call(bf16[8,16,1536]{2,1,0:T(8,128)(2,1)S(1)} %all_to_all.15.recv_ref, f32[8,2,9]{2,1,0:T(2,128)S(1)} %copy-done.1, bf16[16,128]{1,0:T(8,128)(2,1)S(1)} %get-tuple-element.8.near_ref), custom_call_target="tpu_custom_call" | custom-call | tf_op jit(solution)/shard_map/pallas_call | solution.py:285
  16.8 17.6 %all_to_all.16.recv_ref = bf16[16,16,768]{2,1,0:T(8,128)(2,1)S(1)} all-to-all(bf16[16,16,768]{2,1,0:T(8,128)(2,1)S(1)} %shard_map.47.own_ref), channel_id=1, replica_groups=mesh['swath'=8,'seg'=16] {'seg'}, dimensions={0} | all-to-all | bytes 786432 | tf_op jit(solution)/shard_map/all_to_all | solution.py:334
  34.4 0.3 shard_map.48
  34.7 14.8 %all_to_all.17.near_ref = bf16[32,16,640]{2,1,0:T(8,128)(2,1)S(1)} all-to-all(bf16[32,16,640]{2,1,0:T(8,128)(2,1)S(1)} %shard_map.48), channel_id=1, replica_groups=mesh['swath'=8,'seg'=16] {'seg'}, dimensions={0} | all-to-all | bytes 1310720 | tf_op jit(solution)/shard_map/all_to_all | solution.py:336
  49.4 2.8 %shard_map.49 = bf16[4,8,16,1024]{3,2,1,0:T(8,128)(2,1)} custom-call(bf16[16,16,768]{2,1,0:T(8,128)(2,1)S(1)} %shard_map.47.own_ref, bf16[32,16,640]{2,1,0:T(8,128)(2,1)S(1)} %all_to_all.17.near_ref), custom_call_target="tpu_custom_call" | custom-call | tf_op jit(solution)/shard_map/pallas_call | solution.py:315
Async XLA Ops:
  0.0 0.7 %copy-start.3 = (s32[1,16,2]{1,2,0:T(2,128)S(1)}, s32[1,16,2]{1,2,0:T(2,128)}, u32[]{:S(2)}) copy-start(s32[1,16,2]{1,2,0:T(2,128)} %param.7) | copy-start | bytes 388
  0.0 0.7 %copy-start.2 = (s32[1,2,32]{2,1,0:T(2,128)S(1)}, s32[1,2,32]{2,1,0:T(2,128)}, u32[]{:S(2)}) copy-start(s32[1,2,32]{2,1,0:T(2,128)} %param.6) | copy-start | bytes 772
  0.7 0.9 %copy-start = (bf16[1,1,128,1024]{3,2,1,0:T(8,128)(2,1)S(1)}, bf16[1,1,128,1024]{3,2,1,0:T(8,128)(2,1)}, u32[]{:S(2)}) copy-start(bf16[1,1,128,1024]{3,2,1,0:T(8,128)(2,1)} %param.4) | copy-start | bytes 786436
  1.7 13.4 %copy-start.1 = (f32[8,2,9]{2,1,0:T(2,128)S(1)}, f32[8,2,9]{2,1,0:T(2,128)}, u32[]{:S(2)}) copy-start(f32[8,2,9]{2,1,0:T(2,128)} %sten_ref.1) | copy-start | bytes 1732

commit v4 on v3

--- a/solution.py
+++ b/solution.py
@@ -12,6 +12,7 @@
 BLK_C = 128
 NCLASS = 8
 SWATHS = 8
+CORES = 2
 DIES = 16
 ROWS = 128
 COLS = 512
@@ -32,7 +33,8 @@
     return lax.broadcasted_iota(jnp.int32, (count, width), 0)
 
 
-def pack_kernel(band, pix_ref, cls_ref, ids_ref, out_ref, near_ref, row_ref):
+def pack_kernel(band, pix_ref, cls_ref, ids_ref, give_ref, near_ref, *refs):
+    keep_refs, row_ref = refs[:-1], refs[-1]
     if band is None:
         band = lax.axis_index("swath")
     row_ref[...] = jnp.zeros_like(row_ref)
@@ -44,20 +46,27 @@
     row_ref[6:8, 0:COL_BLOCKS] = cls_ref[...].astype(jnp.float32)
     own_classes = row_ref[...]
     sub = rows_of(8, COLS)
-    for piece in range(SWATHS):
-        start = piece * BAND
-        out_ref[piece, :, 0 : CH * COLS] = pix_ref[start : start + BAND, :]
-        halves = []
-        for h in range(CH):
-            lanes = slice(h * COLS, (h + 1) * COLS)
-            above = jnp.zeros((8, COLS), jnp.float32)
-            below = jnp.zeros((8, COLS), jnp.float32)
-            if piece > 0:
-                above = pltpu.roll(pix_ref[start - BAND : start, lanes].astype(jnp.float32)[8:16], 3, 0)
-            if piece < SWATHS - 1:
-                below = pltpu.roll(pix_ref[start + BAND : start + 2 * BAND, lanes].astype(jnp.float32)[0:8], 3, 0)
-            halves.append(jnp.where(sub < 3, above, jnp.where(sub < 6, below, own_classes)))
-        out_ref[piece, :, CH * COLS :] = jnp.concatenate(halves, axis=0).astype(jnp.bfloat16)
+    for turn in range(SWATHS // CORES):
+        for other, target in enumerate((keep_refs[turn], give_ref.at[turn])):
+            piece = ((band // CORES) ^ turn) * CORES + ((band % CORES) ^ other)
+            start = pl.multiple_of(piece * BAND, BAND)
+            before = pl.multiple_of(jnp.maximum(piece - 1, 0) * BAND, BAND)
+            after = pl.multiple_of(jnp.minimum(piece + 1, SWATHS - 1) * BAND, BAND)
+            target[:, 0 : CH * COLS] = pix_ref[pl.ds(start, BAND), :]
+            halves = []
+            for h in range(CH):
+                lanes = slice(h * COLS, (h + 1) * COLS)
+                above = pltpu.roll(pix_ref[pl.ds(before, BAND), lanes].astype(jnp.float32)[8:16], 3, 0)
+                below = pltpu.roll(pix_ref[pl.ds(after, BAND), lanes].astype(jnp.float32)[0:8], 3, 0)
+                above = jnp.where(piece > 0, above, 0.0)
+                below = jnp.where(piece < SWATHS - 1, below, 0.0)
+                halves.append(jnp.where(sub < 3, above, jnp.where(sub < 6, below, own_classes)))
+            target[:, CH * COLS :] = jnp.concatenate(halves, axis=0).astype(jnp.bfloat16)
+
+
+def part_kernel(got_ref, *out_refs):
+    for turn, out_ref in enumerate(out_refs, 1):
+        out_ref[...] = got_ref[turn]
 
 
 def shifter(ref):
@@ -90,15 +99,43 @@
 
 
 def norm_kernel(
-    band, recv_ref, sten_ref, near_ref, out_ref, left_ref, image_ref, right_ref, table_ref
+    band,
+    got_ref,
+    keep_ref,
+    keep_one,
+    keep_two,
+    keep_three,
+    got_one,
+    got_two,
+    got_three,
+    sten_ref,
+    near_ref,
+    out_ref,
+    left_ref,
+    image_ref,
+    right_ref,
+    table_ref,
+    cls_ref,
 ):
     if band is None:
         band = lax.axis_index("swath")
     before = jnp.maximum(band - 1, 0)
     after = jnp.minimum(band + 1, SWATHS - 1)
+    pieces = [(keep_ref, got_ref.at[0]), (keep_one, got_one), (keep_two, got_two), (keep_three, got_three)]
+    for turn, pair in enumerate(pieces):
+        for other, piece in enumerate(pair):
+            source = ((band // CORES) ^ turn) * CORES + ((band % CORES) ^ other)
+            edges = piece[:, CH * COLS :].astype(jnp.float32)
+            cls_ref[source] = edges[0:8, 0:BLK_C]
+            for h in range(CH):
+                halo = pltpu.roll(edges[h * 8 : h * 8 + 8], 5, 0)
+                for q in range(QUADS):
+                    lanes = slice(h * COLS + q * BLK_C, h * COLS + (q + 1) * BLK_C)
+                    rows = piece[:, lanes].astype(jnp.float32)
+                    store_ring(image_ref, h, QUADS * source + q + 1, rows, halo[:, q * BLK_C : (q + 1) * BLK_C])
 
     def class_rows(source):
-        return recv_ref[source, :, CH * COLS : CH * COLS + BLK_C].astype(jnp.float32)[0:8].astype(jnp.int32)
+        return cls_ref[source].astype(jnp.int32)
 
     sub = rows_of(8, BLK_C)
     mine = class_rows(band)
@@ -117,13 +154,6 @@
 
     near = near_ref[...]
     shifted = shifter(image_ref)
-    for g in range(SWATHS):
-        for h in range(CH):
-            halo = pltpu.roll(recv_ref[g, :, CH * COLS :].astype(jnp.float32)[h * 8 : h * 8 + 8], 5, 0)
-            for q in range(QUADS):
-                lanes = slice(h * COLS + q * BLK_C, h * COLS + (q + 1) * BLK_C)
-                rows = recv_ref[g, :, lanes].astype(jnp.float32)
-                store_ring(image_ref, h, QUADS * g + q + 1, rows, halo[:, q * BLK_C : (q + 1) * BLK_C])
 
     def shift(g):
         for h in range(CH):
@@ -265,37 +295,50 @@
 PARAMS = pltpu.CompilerParams(vmem_limit_bytes=VMEM_LIMIT)
 
 
+PIECES = jax.ShapeDtypeStruct((SWATHS // CORES, BAND, 3 * COLS), jnp.bfloat16)
+ONE_PIECE = jax.ShapeDtypeStruct((BAND, 3 * COLS), jnp.bfloat16)
+
+
 def pack(pixels, classes, near, band=None, interpret=False):
     return pl.pallas_call(
         functools.partial(pack_kernel, band),
-        out_shape=(
-            jax.ShapeDtypeStruct((SWATHS, BAND, 3 * COLS), jnp.bfloat16),
-            jax.ShapeDtypeStruct((16, BLK_C), jnp.bfloat16),
-        ),
+        out_shape=(PIECES, jax.ShapeDtypeStruct((16, BLK_C), jnp.bfloat16), *[ONE_PIECE] * 4),
         in_specs=[VMEM] * 3,
-        out_specs=(VMEM,) * 2,
+        out_specs=(VMEM,) * 6,
         scratch_shapes=[pltpu.VMEM((8, COLS), jnp.float32)],
         compiler_params=PARAMS,
         interpret=interpret,
     )(pixels, classes, near)
 
 
-def norm(recv, stencils, near, band=None, interpret=False):
+def part(got, interpret=False):
+    return pl.pallas_call(
+        part_kernel,
+        out_shape=(ONE_PIECE,) * 3,
+        in_specs=[VMEM],
+        out_specs=(VMEM,) * 3,
+        compiler_params=PARAMS,
+        interpret=interpret,
+    )(got)
+
+
+def norm(got, pieces, stencils, near, band=None, interpret=False):
     image = pltpu.VMEM((CH, TILES, 32, BLK_C), jnp.float32)
     return pl.pallas_call(
         functools.partial(norm_kernel, band),
         out_shape=jax.ShapeDtypeStruct((PARTS, BAND, SENT), jnp.bfloat16),
-        in_specs=[VMEM, VMEM, VMEM],
+        in_specs=[VMEM] * 10,
         out_specs=VMEM,
         scratch_shapes=[
             image,
             image,
             image,
             pltpu.VMEM((NCLASS + 1, CH * 9, 8, BLK_C), jnp.float32),
+            pltpu.VMEM((SWATHS, 8, BLK_C), jnp.float32),
         ],
         compiler_params=PARAMS,
         interpret=interpret,
-    )(recv, stencils, near)
+    )(got, *pieces, stencils, near)
 
 
 def pick(recv, interpret=False):
@@ -328,9 +371,15 @@
 
 
 def shards(swath_pixels, stencils, classes, neighbours):
-    packed, near = pack(swath_pixels[0, 0], classes[0], neighbours[0].T)
-    bands = lax.all_to_all(packed, "swath", split_axis=0, concat_axis=0, tiled=True)
-    own = norm(bands, stencils, near)
+    give, near, *keep = pack(swath_pixels[0, 0], classes[0], neighbours[0].T)
+    got = lax.ppermute(give, "swath", [(i, i ^ 1) for i in range(SWATHS)])
+
+    def along_y(piece, turn):
+        return lax.ppermute(piece, "swath", [(i, i ^ (CORES * turn)) for i in range(SWATHS)])
+
+    moved = [along_y(keep[turn], turn) for turn in range(1, 4)]
+    moved += [along_y(piece, turn) for turn, piece in enumerate(part(got), 1)]
+    own = norm(got, [keep[0], *moved], stencils, near)
     pieces = lax.all_to_all(own, "seg", split_axis=0, concat_axis=0, tiled=True)
     picked = pick(pieces)
     references = lax.all_to_all(picked, "seg", split_axis=0, concat_axis=0, tiled=True)

time: 52.5 us -> 52.4 us (level)
  blocking collectives: 45.8 us -> 30.8 us
  starting transfers between devices: 0 us -> 9.64 us
  waiting for transfers between devices: 0 us -> 5.17 us
    all_to_all x1 -> x0, blocking collectives: 13.4 us -> none  [shards(): lax.all_to_all(packed, 'swath', split_axis=0, concat_axis=0, tiled=True)]
    ppermute x0 -> x7, starting transfers between devices: none -> 9.64 us  [the longest x6 9.56 us: along_y(): lax.ppermute(piece, 'swath', [(i, i ^ CORES * turn) for i in range(SWATHS)])]
    ppermute x0 -> x7, waiting for transfers between devices: none -> 5.17 us  [the longest x6 5.16 us: along_y(): lax.ppermute(piece, 'swath', [(i, i ^ CORES * turn) for i in range(SWATHS)])]
    all_to_all x1, blocking collectives: 14.8 us -> 13.7 us  [shards(): lax.all_to_all(picked, 'seg', split_axis=0, concat_axis=0, tiled=True)]
    all_to_all x1, blocking collectives: 17.6 us -> 17.1 us  [shards(): pieces = lax.all_to_all(own, 'seg', split_axis=0, concat_axis=0, tiled=True)]
  transfers between devices with their start and end apart: 0 -> 7, of which waited for: 0 -> 3; matrix products, arithmetic and copies ran while one was open for 0% -> 0% of each run, Pallas kernels for 0% -> 0%
where the time goes in v4:
time: 52.4 us; the launch traced here: 52.2 us
  blocking collectives  30.8 us (59%)
  starting transfers between devices  9.64 us (18%)
  waiting for transfers between devices  5.17 us (10%)
  Pallas kernels  4.84 us (9%)
  local copies, waits for them, and re-layouts  1.65 us (3%)
    all_to_all x1, blocking collectives, shards(): pieces = lax.all_to_all(own, 'seg', split_axis=0, concat_axis=0, tiled=True)  17.1 us
    all_to_all x1, blocking collectives, shards(): lax.all_to_all(picked, 'seg', split_axis=0, concat_axis=0, tiled=True)  13.7 us
    ppermute x6, starting transfers between devices, along_y(): lax.ppermute(piece, 'swath', [(i, i ^ CORES * turn) for i in range(SWATHS)])  9.56 us
    ppermute x6, waiting for transfers between devices, along_y(): lax.ppermute(piece, 'swath', [(i, i ^ CORES * turn) for i in range(SWATHS)])  5.16 us
    pallas_call x1, Pallas kernels, filters(): pl.pallas_call(filter_kernel, out_shape=jax.ShapeDtypeStruct((4, SWATHS,...  2.81 us
    pallas_call x1, Pallas kernels, norm(): pl.pallas_call(functools.partial(norm_kernel, band), out_shape=jax.ShapeD...  1.66 us
    unnamed x8, local copies, waits for them, and re-layouts  1.65 us
  transfers between devices with their start and end apart: 7, of which 3 were waited for; matrix products, arithmetic and copies ran while one was open for 0% of the time, Pallas kernels for 0%

profile of v4, /device:TPU:0, one launch (start us, length us, event | category | flops | bytes accessed | tf_op | source)
XLA Modules:
  0.0 52.2 jit_solution(4844807300086889848)
XLA Ops:
  0.0 0.0 copy-start.3
  0.0 0.0 copy-start.2
  0.0 0.7 %copy-done.3 = s32[1,16,2]{1,2,0:T(2,128)S(1)} copy-done((s32[1,16,2]{1,2,0:T(2,128)S(1)}, s32[1,16,2]{1,2,0:T(2,128)}, u32[]{:S(2)}) %copy-start.3) | copy-done | bytes 152
  0.7 0.0 copy-done.2
  0.7 0.0 copy-start
  0.7 0.9 %copy-done = bf16[1,1,128,1024]{3,2,1,0:T(8,128)(2,1)S(1)} copy-done((bf16[1,1,128,1024]{3,2,1,0:T(8,128)(2,1)S(1)}, bf16[1,1,128,1024]{3,2,1,0:T(8,128)(2,1)}, u32[]{:S(2)}) %copy-start) | copy-done | bytes 262168
  1.6 0.1 shard_map.46
  1.8 0.1 collective-permute-start
  1.8 1.7 %collective-permute-start.1 = (bf16[16,1536]{1,0:T(8,128)(2,1)S(1)}, bf16[16,1536]{1,0:T(8,128)(2,1)S(1)}, u32[]{:S(2)}, u32[]{:S(2)}) collective-permute-start(bf16[16,1536]{1,0:T(8,128)(2,1)S(1)} %get-tuple-element.16), channel_id=1, source_target_pairs={{0,32},{16,48},{32,0},{48,16},{64,96},{80,112},{96,64},{112,80},{1... | collective-permute-start | bytes 147464 | tf_op jit(solution)/shard_map/ppermute | solution.py:378
  3.6 2.9 %collective-permute-start.2 = (bf16[16,1536]{1,0:T(8,128)(2,1)S(1)}, bf16[16,1536]{1,0:T(8,128)(2,1)S(1)}, u32[]{:S(2)}, u32[]{:S(2)}) collective-permute-start(bf16[16,1536]{1,0:T(8,128)(2,1)S(1)} %get-tuple-element.17), channel_id=1, source_target_pairs={{0,64},{16,80},{32,96},{48,112},{64,0},{80,16},{96,32},{112,48},{1... | collective-permute-start | bytes 147464 | tf_op jit(solution)/shard_map/ppermute | solution.py:378
  6.5 0.1 collective-permute-start.3
  6.6 0.0 collective-permute-done.got_ref
  6.6 0.0 copy-start.1
  6.7 0.5 %collective-permute-start.4 = (bf16[16,1536]{1,0:T(8,128)(2,1)S(1)}, bf16[16,1536]{1,0:T(8,128)(2,1)S(1)}, u32[]{:S(2)}, u32[]{:S(2)}) collective-permute-start(bf16[16,1536]{1,0:T(8,128)(2,1)S(1)} %get-tuple-element.19), channel_id=1, source_target_pairs={{0,32},{16,48},{32,0},{48,16},{64,96},{80,112},{96,64},{112,80},{1... | collective-permute-start | bytes 147464 | tf_op jit(solution)/shard_map/ppermute | solution.py:378
  7.2 4.1 %collective-permute-start.5 = (bf16[16,1536]{1,0:T(8,128)(2,1)S(1)}, bf16[16,1536]{1,0:T(8,128)(2,1)S(1)}, u32[]{:S(2)}, u32[]{:S(2)}) collective-permute-start(bf16[16,1536]{1,0:T(8,128)(2,1)S(1)} %get-tuple-element.20), channel_id=1, source_target_pairs={{0,64},{16,80},{32,96},{48,112},{64,0},{80,16},{96,32},{112,48},{1... | collective-permute-start | bytes 147464 | tf_op jit(solution)/shard_map/ppermute | solution.py:378
  11.3 0.0 collective-permute-done.1.keep_one
  11.3 0.1 collective-permute-start.6
  11.4 0.0 collective-permute-done.2.keep_two
  11.4 0.3 collective-permute-done.3.keep_three
  11.8 0.0 collective-permute-done.4.got_one
  11.8 2.1 %collective-permute-done.5.got_two = bf16[16,1536]{1,0:T(8,128)(2,1)S(1)} collective-permute-done((bf16[16,1536]{1,0:T(8,128)(2,1)S(1)}, bf16[16,1536]{1,0:T(8,128)(2,1)S(1)}, u32[]{:S(2)}, u32[]{:S(2)}) %collective-permute-start.5) | collective-permute-done | bytes 49184 | tf_op jit(solution)/shard_map/ppermute | solution.py:378
  13.9 2.7 %collective-permute-done.6.got_three = bf16[16,1536]{1,0:T(8,128)(2,1)S(1)} collective-permute-done((bf16[16,1536]{1,0:T(8,128)(2,1)S(1)}, bf16[16,1536]{1,0:T(8,128)(2,1)S(1)}, u32[]{:S(2)}, u32[]{:S(2)}) %collective-permute-start.6) | collective-permute-done | bytes 49184 | tf_op jit(solution)/shard_map/ppermute | solution.py:378
  16.6 0.0 copy-done.1
  16.6 1.7 %shard_map.48.own_ref = bf16[16,16,768]{2,1,0:T(8,128)(2,1)S(1)} custom-call(bf16[4,16,1536]{2,1,0:T(8,128)(2,1)S(1)} %collective-permute-done.got_ref, bf16[16,1536]{1,0:T(8,128)(2,1)S(1)} %get-tuple-element.15.keep_ref, bf16[16,1536]{1,0:T(8,128)(2,1)S(1)} %collective-permute-done.1.keep_one, bf16[16,1536]{1,0:T(8,128)(2,1)S(1)} %collective-permute-done.2.keep_two, ...), custom_call_target="tpu_custom_call" | custom-call | tf_op jit(solution)/shard_map/pallas_call | solution.py:327
  18.3 17.1 %all_to_all.10.recv_ref = bf16[16,16,768]{2,1,0:T(8,128)(2,1)S(1)} all-to-all(bf16[16,16,768]{2,1,0:T(8,128)(2,1)S(1)} %shard_map.48.own_ref), channel_id=1, replica_groups=mesh['swath'=8,'seg'=16] {'seg'}, dimensions={0} | all-to-all | bytes 786432 | tf_op jit(solution)/shard_map/all_to_all | solution.py:383
  35.4 0.3 shard_map.49
  35.6 13.7 %all_to_all.11.near_ref = bf16[32,16,640]{2,1,0:T(8,128)(2,1)S(1)} all-to-all(bf16[32,16,640]{2,1,0:T(8,128)(2,1)S(1)} %shard_map.49), channel_id=1, replica_groups=mesh['swath'=8,'seg'=16] {'seg'}, dimensions={0} | all-to-all | bytes 1310720 | tf_op jit(solution)/shard_map/all_to_all | solution.py:385
  49.4 2.8 %shard_map.50 = bf16[4,8,16,1024]{3,2,1,0:T(8,128)(2,1)} custom-call(bf16[16,16,768]{2,1,0:T(8,128)(2,1)S(1)} %shard_map.48.own_ref, bf16[32,16,640]{2,1,0:T(8,128)(2,1)S(1)} %all_to_all.11.near_ref), custom_call_target="tpu_custom_call" | custom-call | tf_op jit(solution)/shard_map/pallas_call | solution.py:358
  (1 shorter events, 0.0 us)
Async XLA Ops:
  0.0 0.7 %copy-start.3 = (s32[1,16,2]{1,2,0:T(2,128)S(1)}, s32[1,16,2]{1,2,0:T(2,128)}, u32[]{:S(2)}) copy-start(s32[1,16,2]{1,2,0:T(2,128)} %param.7) | copy-start | bytes 388
  0.0 0.7 %copy-start.2 = (s32[1,2,32]{2,1,0:T(2,128)S(1)}, s32[1,2,32]{2,1,0:T(2,128)}, u32[]{:S(2)}) copy-start(s32[1,2,32]{2,1,0:T(2,128)} %param.6) | copy-start | bytes 772
  0.7 0.9 %copy-start = (bf16[1,1,128,1024]{3,2,1,0:T(8,128)(2,1)S(1)}, bf16[1,1,128,1024]{3,2,1,0:T(8,128)(2,1)}, u32[]{:S(2)}) copy-start(bf16[1,1,128,1024]{3,2,1,0:T(8,128)(2,1)} %param.4) | copy-start | bytes 786436
  1.8 4.9 %collective-permute-start = (bf16[4,16,1536]{2,1,0:T(8,128)(2,1)S(1)}, bf16[4,16,1536]{2,1,0:T(8,128)(2,1)S(1)}, u32[]{:S(2)}, u32[]{:S(2)}) collective-permute-start(bf16[4,16,1536]{2,1,0:T(8,128)(2,1)S(1)} %get-tuple-element.14), channel_id=1, source_target_pairs={{0,16},{16,0},{32,48},{48,32},{64,80},{80,64},{96,112},{112,96},{1... | collective-permute-start | bytes 589832 | tf_op jit(solution)/shard_map/ppermute | solution.py:375
  1.8 9.5 %collective-permute-start.1 = (bf16[16,1536]{1,0:T(8,128)(2,1)S(1)}, bf16[16,1536]{1,0:T(8,128)(2,1)S(1)}, u32[]{:S(2)}, u32[]{:S(2)}) collective-permute-start(bf16[16,1536]{1,0:T(8,128)(2,1)S(1)} %get-tuple-element.16), channel_id=1, source_target_pairs={{0,32},{16,48},{32,0},{48,16},{64,96},{80,112},{96,64},{112,80},{1... | collective-permute-start | bytes 147464 | tf_op jit(solution)/shard_map/ppermute | solution.py:378
  3.6 7.9 %collective-permute-start.2 = (bf16[16,1536]{1,0:T(8,128)(2,1)S(1)}, bf16[16,1536]{1,0:T(8,128)(2,1)S(1)}, u32[]{:S(2)}, u32[]{:S(2)}) collective-permute-start(bf16[16,1536]{1,0:T(8,128)(2,1)S(1)} %get-tuple-element.17), channel_id=1, source_target_pairs={{0,64},{16,80},{32,96},{48,112},{64,0},{80,16},{96,32},{112,48},{1... | collective-permute-start | bytes 147464 | tf_op jit(solution)/shard_map/ppermute | solution.py:378
  6.5 5.3 %collective-permute-start.3 = (bf16[16,1536]{1,0:T(8,128)(2,1)S(1)}, bf16[16,1536]{1,0:T(8,128)(2,1)S(1)}, u32[]{:S(2)}, u32[]{:S(2)}) collective-permute-start(bf16[16,1536]{1,0:T(8,128)(2,1)S(1)} %get-tuple-element.18), channel_id=1, source_target_pairs={{0,96},{16,112},{32,64},{48,80},{64,32},{80,48},{96,0},{112,16},{1... | collective-permute-start | bytes 147464 | tf_op jit(solution)/shard_map/ppermute | solution.py:378
  6.6 10.0 %copy-start.1 = (f32[8,2,9]{2,1,0:T(2,128)S(1)}, f32[8,2,9]{2,1,0:T(2,128)}, u32[]{:S(2)}) copy-start(f32[8,2,9]{2,1,0:T(2,128)} %sten_ref.1) | copy-start | bytes 1732
  6.7 5.1 %collective-permute-start.4 = (bf16[16,1536]{1,0:T(8,128)(2,1)S(1)}, bf16[16,1536]{1,0:T(8,128)(2,1)S(1)}, u32[]{:S(2)}, u32[]{:S(2)}) collective-permute-start(bf16[16,1536]{1,0:T(8,128)(2,1)S(1)} %get-tuple-element.19), channel_id=1, source_target_pairs={{0,32},{16,48},{32,0},{48,16},{64,96},{80,112},{96,64},{112,80},{1... | collective-permute-start | bytes 147464 | tf_op jit(solution)/shard_map/ppermute | solution.py:378
  7.2 6.7 %collective-permute-start.5 = (bf16[16,1536]{1,0:T(8,128)(2,1)S(1)}, bf16[16,1536]{1,0:T(8,128)(2,1)S(1)}, u32[]{:S(2)}, u32[]{:S(2)}) collective-permute-start(bf16[16,1536]{1,0:T(8,128)(2,1)S(1)} %get-tuple-element.20), channel_id=1, source_target_pairs={{0,64},{16,80},{32,96},{48,112},{64,0},{80,16},{96,32},{112,48},{1... | collective-permute-start | bytes 147464 | tf_op jit(solution)/shard_map/ppermute | solution.py:378
  11.3 5.3 %collective-permute-start.6 = (bf16[16,1536]{1,0:T(8,128)(2,1)S(1)}, bf16[16,1536]{1,0:T(8,128)(2,1)S(1)}, u32[]{:S(2)}, u32[]{:S(2)}) collective-permute-start(bf16[16,1536]{1,0:T(8,128)(2,1)S(1)} %get-tuple-element.21), channel_id=1, source_target_pairs={{0,96},{16,112},{32,64},{48,80},{64,32},{80,48},{96,0},{112,16},{1... | collective-permute-start | bytes 147464 | tf_op jit(solution)/shard_map/ppermute | solution.py:378
